TPU v7x, 32 devices: a whole 2x2x4 slice. The times are simulated.
32 devices in a mesh: lat: 4 (over z), lon: 2 (over x), chan: 4 (over y, core).
Axes of the slice: x: 2, y: 2, z: 4, core: 2. Of those that a mesh axis runs over, the one named last changes fastest.
Arguments:
- queries: bfloat16 [64, 16, 2560], P('lat', 'lon', 'chan'), may hold values from -8 to 8
- keys: bfloat16 [64, 16, 2560], P('lat', 'lon', 'chan'), may hold values from -8 to 8
- values: bfloat16 [64, 16, 2560], P('lat', 'lon', 'chan'), may hold values from -6 to 6
- attn_out: bfloat16 [64, 16, 2560], P('lat', 'lon', 'chan'), may hold values from -6 to 6
- grad_out: bfloat16 [64, 16, 5120], P('lat', 'lon', 'chan'), may hold values from -6 to 6
- w_out: bfloat16 [5120, 2560], P(('lat', 'lon'), 'chan'), may hold values from -0.078125 to 0.078125
- bias_table: float32 [20, 25, 13], P('chan'), may hold values from -5 to 5
- key_mask: int32 [64, 16], replicated, may hold values 0 or 1
Outputs:
- grad_queries: bfloat16 [64, 16, 2560], P('lat', 'lon', 'chan')
- grad_keys: bfloat16 [64, 16, 2560], P('lat', 'lon', 'chan')
- grad_values: bfloat16 [64, 16, 2560], P('lat', 'lon', 'chan')
- grad_wout: float32 [5120, 2560], P(('lat', 'lon'), 'chan')
- grad_table: float32 [20, 25, 13], P('chan')
All inputs are finite; a program needn't handle non-finite values.
Results may differ from a plain program's by a relative error of at most 0.007.
Values may be sent and summed in bfloat16 or wider, within the bound.
A program may use at most 128 MiB of HBM per device.

v0:
```python
import jax
import jax.numpy as jnp
from jax import lax
from jax.sharding import PartitionSpec as P

HEAD_DIM = 128
WIN = 13


def extended_2(value, sides, width, wrap):
    for axis, dim in sides:
        count, length = (lax.axis_size(axis), value.shape[dim])
        up = [(i, (i + 1) % count) for i in range(count if wrap else count - 1)]
        down = [(j, i) for i, j in up]
        last = lax.slice_in_dim(value, length - width, length, axis=dim)
        leading = lax.slice_in_dim(value, 0, width, axis=dim)
        before = lax.ppermute(last, axis, up)
        after = lax.ppermute(leading, axis, down)
        value = jnp.concatenate([before, value, after], axis=dim)
    return value


def fold_lon(extended, core_width):
    full_width = extended.shape[2]
    reach_cells = (full_width - core_width) // 2
    rim_cells = jnp.concatenate(
        [extended[:, :, :reach_cells], extended[:, :, full_width - reach_cells :]], axis=2
    )
    received = extended_2(rim_cells.astype(jnp.bfloat16), (("lon", 2),), reach_cells, True).astype(
        rim_cells.dtype
    )
    middle = extended[:, :, reach_cells : full_width - reach_cells]
    front_add = jnp.pad(
        received[:, :, :reach_cells], ((0, 0), (0, 0), (0, core_width - reach_cells), (0, 0))
    )
    back_add = jnp.pad(
        received[:, :, 3 * reach_cells :], ((0, 0), (0, 0), (core_width - reach_cells, 0), (0, 0))
    )
    return middle + front_add + back_add


def fold_lat(extended, core_width):
    full_width = extended.shape[1]
    reach_cells = (full_width - core_width) // 2
    rim_cells = jnp.concatenate(
        [extended[:, :reach_cells], extended[:, full_width - reach_cells :]], axis=1
    )
    received = extended_2(rim_cells.astype(jnp.bfloat16), (("lat", 1),), reach_cells, False).astype(
        rim_cells.dtype
    )
    middle = extended[:, reach_cells : full_width - reach_cells]
    front_add = jnp.pad(
        received[:, :reach_cells], ((0, 0), (0, core_width - reach_cells), (0, 0), (0, 0))
    )
    back_add = jnp.pad(
        received[:, 3 * reach_cells :], ((0, 0), (core_width - reach_cells, 0), (0, 0), (0, 0))
    )
    return middle + front_add + back_add


def local(queries, keys, values, attn_out, grad_out, w_out, bias_table, key_mask):
    lat_rows, lon_cols, chan_width = queries.shape
    head_count = bias_table.shape[0]
    reach_cells = WIN // 2
    score_scale = HEAD_DIM ** (-0.5)
    tokens = lat_rows * lon_cols
    ext_rows = lat_rows + 2 * reach_cells
    ext_cols = lon_cols + 2 * reach_cells
    row_block = 4
    key_span = row_block + WIN - 1
    block_count = lat_rows // row_block
    block_rows = row_block * lon_cols
    block_keys = key_span * ext_cols
    offset_rows = 2 * WIN - 1
    low_pad = row_block - 1
    lat_total = lat_rows * lax.axis_size("lat")
    lon_total = lon_cols * lax.axis_size("lon")
    contract_lead = (((0,), (0,)), ((), ()))
    full_grad = lax.all_gather(grad_out, "chan", axis=2, tiled=True).reshape(tokens, -1)
    grad_cols = jnp.transpose(full_grad)
    slab_part = grad_cols
    grad_attn = lax.dot_general(
        slab_part,
        lax.all_gather(w_out, ("lat", "lon"), axis=0, tiled=True),
        contract_lead,
        preferred_element_type=jnp.float32,
    ).astype(jnp.bfloat16)
    kv_pair = jnp.stack([keys, values])
    extended = extended_2(kv_pair, (("lat", 1), ("lon", 2)), reach_cells, True)
    lat_first = lax.axis_index("lat") * lat_rows
    lon_first = lax.axis_index("lon") * lon_cols
    ext_col = lon_first - reach_cells + jnp.arange(ext_cols, dtype=jnp.int32)
    wrap_col = ext_col % lon_total
    mask_cols = jnp.take(key_mask, wrap_col, axis=1)
    mark_cols = wrap_col % 4 == 0
    rel_lon = (
        jnp.arange(ext_cols, dtype=jnp.int32)[None, :]
        - jnp.arange(lon_cols, dtype=jnp.int32)[:, None]
    )
    in_lon = (rel_lon >= 0) & (rel_lon < WIN)
    lon_pick = jnp.clip(rel_lon, 0, WIN - 1)
    lon_table = jnp.take(bias_table, lon_pick, axis=2).transpose(0, 2, 1, 3)
    table_pad = jnp.pad(lon_table, ((0, 0), (0, 0), (low_pad, low_pad), (0, 0)))
    query_heads = queries.reshape(lat_rows, lon_cols, head_count, HEAD_DIM)
    grad_heads = grad_attn.reshape(lat_rows, lon_cols, head_count, HEAD_DIM)

    def block_step(state_pair, block_index):
        grad_pair, table_acc = state_pair
        local_first = block_index * row_block
        top_row = lat_first + local_first
        key_first = jnp.clip(top_row - reach_cells, 0, lat_total - key_span)
        key_local = key_first - (lat_first - reach_cells)
        query_rows = top_row + jnp.arange(row_block, dtype=jnp.int32)
        window_first = jnp.clip(query_rows - reach_cells, 0, lat_total - WIN)
        key_glob = key_first + jnp.arange(key_span, dtype=jnp.int32)
        in_lat = (key_glob[None, :] >= window_first[:, None]) & (
            key_glob[None, :] < window_first[:, None] + WIN
        )
        mask_rows = lax.dynamic_slice_in_dim(mask_cols, key_first, key_span, 0)
        valid_keys = (mask_rows == 1) | (key_glob % 4 == 0)[:, None] & mark_cols[None, :]
        allowed = in_lat[:, None, :, None] & in_lon[None, :, None, :] & valid_keys[None, None, :, :]
        allowed = allowed.reshape(block_rows, block_keys)
        shifts = key_first - query_rows + (WIN - 1) + low_pad
        bias_parts = [
            lax.dynamic_slice_in_dim(table_pad, shifts[row_pos], key_span, 2)
            for row_pos in range(row_block)
        ]
        bias_rows = jnp.stack(bias_parts, axis=1).reshape(head_count, block_rows, block_keys)
        query_block = lax.dynamic_slice_in_dim(query_heads, local_first, row_block, 0).reshape(
            block_rows, head_count, HEAD_DIM
        )
        grad_block = lax.dynamic_slice_in_dim(grad_heads, local_first, row_block, 0).reshape(
            block_rows, head_count, HEAD_DIM
        )
        pair_block = lax.dynamic_slice_in_dim(extended, key_local, key_span, 1).reshape(
            2, block_keys, head_count, HEAD_DIM
        )
        key_block = pair_block[0]
        value_block = pair_block[1]
        scores = (
            score_scale
            * jnp.einsum("qhd,khd->hqk", query_block, key_block, preferred_element_type=jnp.float32)
            + bias_rows
        )
        scores = jnp.where(allowed[None], scores, -1e30)
        row_max = jnp.max(scores, axis=2, keepdims=True)
        weights_exp = jnp.exp(scores - row_max)
        prob_rows = weights_exp / jnp.sum(weights_exp, axis=2, keepdims=True)
        grad_prob = jnp.einsum(
            "qhd,khd->hqk", grad_block, value_block, preferred_element_type=jnp.float32
        )
        row_delta = jnp.sum(prob_rows * grad_prob, axis=2, keepdims=True)
        dscore = prob_rows * (grad_prob - row_delta)
        score_grid = dscore.reshape(head_count, row_block, lon_cols, key_span, ext_cols)
        score_grid = score_grid.transpose(0, 1, 3, 2, 4).reshape(
            head_count, row_block, key_span, lon_cols * ext_cols
        )
        for row_pos in range(row_block):
            prior_sum = lax.dynamic_slice_in_dim(table_acc, shifts[row_pos], key_span, 1)
            table_acc = lax.dynamic_update_slice_in_dim(
                table_acc, prior_sum + score_grid[:, row_pos], shifts[row_pos], 1
            )
        dscore_low = dscore.astype(jnp.bfloat16)
        prob_low = prob_rows.astype(jnp.bfloat16)
        grad_query = (
            score_scale
            * jnp.einsum("hqk,khd->qhd", dscore_low, key_block, preferred_element_type=jnp.float32)
        ).astype(jnp.bfloat16)
        key_part = score_scale * jnp.einsum(
            "hqk,qhd->khd", dscore_low, query_block, preferred_element_type=jnp.float32
        )
        value_part = jnp.einsum(
            "hqk,qhd->khd", prob_low, grad_block, preferred_element_type=jnp.float32
        )
        new_part = jnp.stack([key_part, value_part]).reshape(2, key_span, ext_cols, chan_width)
        prior_pair = lax.dynamic_slice_in_dim(grad_pair, key_local, key_span, 1)
        grad_pair = lax.dynamic_update_slice_in_dim(grad_pair, prior_pair + new_part, key_local, 1)
        return ((grad_pair, table_acc), grad_query)

    zero_pair = jnp.zeros((2, ext_rows, ext_cols, chan_width), jnp.float32)
    zero_table = jnp.zeros(
        (head_count, offset_rows + 2 * low_pad, lon_cols * ext_cols), jnp.float32
    )
    (grad_pair, table_acc), query_blocks = lax.scan(
        block_step, (zero_pair, zero_table), jnp.arange(block_count, dtype=jnp.int32)
    )
    grad_queries = query_blocks.reshape(lat_rows, lon_cols, chan_width)
    table_core = table_acc[:, low_pad : low_pad + offset_rows].reshape(
        head_count, offset_rows, lon_cols, ext_cols
    )
    col_take = (
        jnp.arange(lon_cols, dtype=jnp.int32)[:, None] + jnp.arange(WIN, dtype=jnp.int32)[None, :]
    )
    col_take = jnp.broadcast_to(
        col_take[None, None, :, :], (head_count, offset_rows, lon_cols, WIN)
    )
    table_local = jnp.sum(jnp.take_along_axis(table_core, col_take, axis=3), axis=2)
    grad_table = lax.psum(table_local, ("lat", "lon"))
    folded = fold_lat(fold_lon(grad_pair, lon_cols), lat_rows)
    grad_keys = folded[0].astype(jnp.bfloat16)
    grad_values = folded[1].astype(jnp.bfloat16)
    saved_out = attn_out.reshape(tokens, chan_width)
    slab_part = grad_cols
    grad_wout = lax.psum_scatter(
        jnp.dot(slab_part, saved_out, preferred_element_type=jnp.float32),
        ("lat", "lon"),
        scatter_dimension=0,
        tiled=True,
    )
    return (grad_queries, grad_keys, grad_values, grad_wout, grad_table)


def solution(mesh):
    return jax.shard_map(
        local,
        mesh=mesh,
        in_specs=(
            P("lat", "lon", "chan"),
            P("lat", "lon", "chan"),
            P("lat", "lon", "chan"),
            P("lat", "lon", "chan"),
            P("lat", "lon", "chan"),
            P(("lat", "lon"), "chan"),
            P("chan", None, None),
            P(),
        ),
        out_specs=(
            P("lat", "lon", "chan"),
            P("lat", "lon", "chan"),
            P("lat", "lon", "chan"),
            P(("lat", "lon"), "chan"),
            P("chan", None, None),
        ),
        check_vma=False,
    )
```

profile of v0, /device:TPU:12, one launch (start us, length us, event | category | flops | bytes accessed | tf_op | source)
XLA Modules:
  0.0 474.2 jit_solution(3824357107013028894)
XLA Ops:
  7.2 1.8 copy.63
  9.1 0.7 all-gather.5.cloned.1.call-update
  9.8 18.7 %all-gather.3.cloned.1.call-done = bf16[16,8,5120]{2,0,1:T(8,128)(2,1)} async-done(((bf16[16,8,1280]{2,0,1:T(8,128)(2,1)}), bf16[16,8,5120]{2,0,1:T(8,128)(2,1)}) %all-gather.3.cloned.1.call-update) | async-done | bytes 1310736 | tf_op jit(solution)/shard_map/all_gather | solution.py:79
  28.6 7.9 %convolution_bitcast_fusion.1 = f32[5120,640]{1,0:T(8,128)} fusion(bf16[16,8,5120]{2,0,1:T(8,128)(2,1)} %all-gather.3.cloned.1.call-done, bf16[16,8,640]{2,1,0:T(8,128)(2,1)S(1)} %copy-done), kind=kOutput, calls=%fused_computation.77 | convolution fusion | flops 838860800 | bytes 14581760 | tf_op jit(solution)/shard_map/dot_general | solution.py:205
  36.5 0.9 copy-done.10
  37.5 1.5 collective-permute-start
  40.5 4.9 %collective-permute-done = bf16[2,6,8,640]{3,2,1,0:T(8,128)(2,1)S(1)} collective-permute-done((bf16[2,6,8,640]{3,2,1,0:T(8,128)(2,1)S(1)}, bf16[2,6,8,640]{3,2,1,0:T(8,128)(2,1)S(1)}, u32[]{:S(2)}, u32[]{:S(2)}) %collective-permute-start) | collective-permute-done | bytes 122912 | tf_op jit(solution)/shard_map/ppermute | solution.py:17
  45.4 6.9 %collective-permute-done.1 = bf16[2,6,8,640]{3,2,1,0:T(8,128)(2,1)S(1)} collective-permute-done((bf16[2,6,8,640]{3,2,1,0:T(8,128)(2,1)S(1)}, bf16[2,6,8,640]{3,2,1,0:T(8,128)(2,1)S(1)}, u32[]{:S(2)}, u32[]{:S(2)}) %collective-permute-start.1) | collective-permute-done | bytes 122912 | tf_op jit(solution)/shard_map/ppermute | solution.py:18
  53.2 1.8 collective-permute-start.3
  55.3 1.4 gather_fusion.1
  57.3 0.9 pad.20.clone
  58.3 7.8 %collective-permute-done.3 = bf16[2,28,6,640]{3,0,2,1:T(2,128)(2,1)S(1)} collective-permute-done((bf16[2,28,6,640]{3,0,2,1:T(2,128)(2,1)S(1)}, bf16[2,28,6,640]{3,0,2,1:T(2,128)(2,1)S(1)}, u32[]{:S(2)}, u32[]{:S(2)}) %collective-permute-start.3) | collective-permute-done | bytes 430112 | tf_op jit(solution)/shard_map/ppermute | solution.py:18
  66.1 8.1 %collective-permute-done.2 = bf16[2,28,6,640]{3,0,2,1:T(2,128)(2,1)S(1)} collective-permute-done((bf16[2,28,6,640]{3,0,2,1:T(2,128)(2,1)S(1)}, bf16[2,28,6,640]{3,0,2,1:T(2,128)(2,1)S(1)}, u32[]{:S(2)}, u32[]{:S(2)}) %collective-permute-start.2) | collective-permute-done | bytes 430112 | tf_op jit(solution)/shard_map/ppermute | solution.py:17
  74.3 2.1 pad_maximum_fusion.1
  76.4 59.9 %all-gather.5.cloned.1.call-done = bf16[5120,640]{1,0:T(8,128)(2,1)} async-done(((bf16[640,640]{1,0:T(8,128)(2,1)}), bf16[5120,640]{1,0:T(8,128)(2,1)}) %all-gather.5.cloned.1.call-update) | async-done | bytes 6553616 | tf_op jit(solution)/shard_map/all_gather | solution.py:84
  136.3 5.2 %fusion.42 = bf16[16,8,5,128]{3,1,2,0:T(8,128)(2,1)} fusion(bf16[5120,640]{1,0:T(8,128)(2,1)} %all-gather.5.cloned.1.call-done, bf16[16,8,5120]{2,0,1:T(8,128)(2,1)S(1)} %copy-done.12), kind=kOutput, calls=%fused_computation.86 | convolution fusion | flops 838942720 | bytes 8028160 | tf_op jit(solution)/shard_map/dot_general | solution.py:82
  141.6 1.9 broadcast_in_dim.94
  143.5 112.1 %while.18 = (s32[]{:T(128)}, f32[2,28,20,640]{3,2,1,0:T(8,128)}, f32[5,31,160]{2,1,0:T(8,128)S(1)}, bf16[4,32,5,128]{3,1,2,0:T(8,128)(2,1)S(1)}, s32[4]{0:T(128)...) while((s32[]{:T(128)}, f32[2,28,20,640]{3,2,1,0:T(8,128)}, ...), condition=%wide.region_4.5_spmd.clone, body=%wide.region_0.0_spmd.clone.sunk | while | flops 67648624 | bytes 32796352 | solution.py:184
  153.7 0.8 constant_dynamic-slice_fusion.6
  154.5 1.3 constant_dynamic-slice_fusion.7
  156.7 1.9 dynamic-slice_bitcast_fusion.5
  159.6 0.9 fusion.104
  162.2 1.2 stack.66
  164.3 1.2 stack.67
  165.5 0.8 reshape.367
  168.4 3.0 fusion.106
  181.6 0.8 constant_dynamic-slice_fusion.6
  182.4 1.3 constant_dynamic-slice_fusion.7
  184.7 1.9 dynamic-slice_bitcast_fusion.5
  187.5 0.9 fusion.104
  190.2 1.2 stack.66
  192.2 1.2 stack.67
  193.4 0.8 reshape.367
  196.4 3.0 fusion.106
  209.6 0.8 constant_dynamic-slice_fusion.6
  210.4 1.3 constant_dynamic-slice_fusion.7
  212.6 1.9 dynamic-slice_bitcast_fusion.5
  215.5 0.9 fusion.104
  218.2 1.2 stack.66
  220.2 1.2 stack.67
  221.4 0.8 reshape.367
  224.4 3.1 fusion.106
  237.7 0.8 constant_dynamic-slice_fusion.6
  238.5 1.3 constant_dynamic-slice_fusion.7
  240.7 1.9 dynamic-slice_bitcast_fusion.5
  243.6 0.9 fusion.104
  246.2 1.2 stack.66
  248.3 1.2 stack.67
  249.5 0.8 reshape.367
  252.4 3.1 fusion.106
  255.5 2.4 convert.16
  258.1 1.2 copy.70
  259.3 1.1 copy.71
  261.0 1.4 collective-permute-start.4
  263.5 0.9 reshape.332
  264.6 155.1 %gather_fusion.2 = f32[13000]{0:T(1024)S(1)} fusion(f32[5,25,8,20]{3,2,1,0:T(8,128)S(1)} %reshape.333, s32[13000]{0:T(1024)S(1)} %reshape.350), kind=kCustom, calls=%fused_computation.2 | custom fusion | bytes 312000 | tf_op jit(solution)/shard_map/jit(take_along_axis)/gather | solution.py:197
  420.1 1.1 copy.73
  421.2 1.1 copy.72
  423.0 2.3 fusion.59
  425.3 4.1 collective-permute-start.6
  429.5 1.9 collective-permute-start.7
  431.6 34.3 %psum.7 = f32[5,25,13]{2,1,0:T(8,128)S(1)} all-reduce(f32[5,25,13]{2,1,0:T(8,128)S(1)} %select_reduce_fusion), channel_id=1, replica_groups=mesh['lat'=4,'lon'=2,'chan'=4] {'lat','lon'}, use_global_device_ids=true, to_apply=%region_7.8 | all-reduce | flops 1625 | bytes 13000 | tf_op jit(solution)/shard_map/psum | solution.py:198
  465.9 0.7 copy.75
  466.9 0.8 slice_bitcast_fusion.4
  (265 shorter events, 41.0 us)
Async XLA Ops:
  7.2 21.4 %copy-start = (bf16[16,8,640]{2,1,0:T(8,128)(2,1)S(1)}, bf16[16,8,640]{2,1,0:T(8,128)(2,1)}, u32[]{:S(2)}) copy-start(bf16[16,8,640]{2,1,0:T(8,128)(2,1)} %param.13) | copy-start | bytes 491524
  7.2 21.4 %all-gather.3.cloned.1.call-start = ((), (), s32[]{:S(2)}) async-start(), calls=%async_computation.1 | async-start | bytes 1638400 | tf_op jit(solution)/shard_map/all_gather | solution.py:79
  9.0 127.3 %all-gather.5.cloned.1.call-start = ((), (), s32[]{:S(2)}) async-start(), calls=%async_computation.2 | async-start | bytes 7372800 | tf_op jit(solution)/shard_map/all_gather | solution.py:84
  9.8 457.9 %reduce-scatter.2.cloned.1.call-start = ((), (), s32[]{:S(2)}) async-start(), calls=%async_computation.3 | async-start | bytes 14745600 | tf_op jit(solution)/shard_map/reduce_scatter | solution.py:204
  36.5 0.9 copy-start.10
  36.5 1.0 copy-start.11
  36.5 3.2 copy-start.9
  37.5 7.8 %collective-permute-start = (bf16[2,6,8,640]{3,2,1,0:T(8,128)(2,1)S(1)}, bf16[2,6,8,640]{3,2,1,0:T(8,128)(2,1)S(1)}, u32[]{:S(2)}, u32[]{:S(2)}) collective-permute-start(bf16[2,6,8,640]{3,2,1,0:T(8,128)(2,1)S(1)} %get-tuple-element.367), channel_id=1, source_target_pairs={{0,8},{8,16},{16,24},{24,0},{1,9},{9,17},{17,25},{25,1},{2,10},{10... | collective-permute-start | bytes 368648 | tf_op jit(solution)/shard_map/ppermute | solution.py:17
  39.1 13.2 %collective-permute-start.1 = (bf16[2,6,8,640]{3,2,1,0:T(8,128)(2,1)S(1)}, bf16[2,6,8,640]{3,2,1,0:T(8,128)(2,1)S(1)}, u32[]{:S(2)}, u32[]{:S(2)}) collective-permute-start(bf16[2,6,8,640]{3,2,1,0:T(8,128)(2,1)S(1)} %get-tuple-element.368), channel_id=1, source_target_pairs={{8,0},{16,8},{24,16},{0,24},{9,1},{17,9},{25,17},{1,25},{10,2},{18... | collective-permute-start | bytes 368648 | tf_op jit(solution)/shard_map/ppermute | solution.py:18
  52.3 3.0 copy-start.2
  53.2 12.8 %collective-permute-start.3 = (bf16[2,28,6,640]{3,0,2,1:T(2,128)(2,1)S(1)}, bf16[2,28,6,640]{3,0,2,1:T(2,128)(2,1)S(1)}, u32[]{:S(2)}, u32[]{:S(2)}) collective-permute-start(bf16[2,28,6,640]{3,0,2,1:T(2,128)(2,1)S(1)} %copy.59), channel_id=1, source_target_pairs={{4,0},{0,4},{5,1},{1,5},{6,2},{2,6},{7,3},{3,7},{12,8},{8,12},{13,... | collective-permute-start | bytes 1290248 | tf_op jit(solution)/shard_map/ppermute | solution.py:18
  55.0 19.3 %collective-permute-start.2 = (bf16[2,28,6,640]{3,0,2,1:T(2,128)(2,1)S(1)}, bf16[2,28,6,640]{3,0,2,1:T(2,128)(2,1)S(1)}, u32[]{:S(2)}, u32[]{:S(2)}) collective-permute-start(bf16[2,28,6,640]{3,0,2,1:T(2,128)(2,1)S(1)} %copy.58), channel_id=1, source_target_pairs={{0,4},{4,0},{1,5},{5,1},{2,6},{6,2},{3,7},{7,3},{8,12},{12,8},{9,1... | collective-permute-start | bytes 1290248 | tf_op jit(solution)/shard_map/ppermute | solution.py:17
  74.3 62.0 %copy-start.12 = (bf16[16,8,5120]{2,0,1:T(8,128)(2,1)S(1)}, bf16[16,8,5120]{2,0,1:T(8,128)(2,1)}, u32[]{:S(2)}) copy-start(bf16[16,8,5120]{2,0,1:T(8,128)(2,1)} %all-gather.3.cloned.1.call-done) | copy-start | bytes 3932164
  161.1 2.3 copy-start.13
  166.7 1.5 copy-start.3
  167.1 1.3 copy-start.4
  168.4 3.0 copy-start.14
  189.1 2.3 copy-start.13
  194.7 1.5 copy-start.3
  195.1 1.3 copy-start.4
  196.4 3.0 copy-start.14
  217.1 2.3 copy-start.13
  222.7 1.5 copy-start.3
  223.1 1.3 copy-start.4
  224.4 3.1 copy-start.14
  245.1 2.3 copy-start.13
  250.7 1.5 copy-start.3
  251.1 1.3 copy-start.4
  252.4 3.1 copy-start.14
  258.1 4.3 copy-start.5
  258.1 4.3 copy-start.7
  260.4 159.7 %collective-permute-start.5 = (bf16[2,28,6,640]{3,0,2,1:T(2,128)(2,1)}, bf16[2,28,6,640]{3,0,2,1:T(2,128)(2,1)}, u32[]{:S(2)}, u32[]{:S(2)}) collective-permute-start(bf16[2,28,6,640]{3,0,2,1:T(2,128)(2,1)} %copy.71), channel_id=1, source_target_pairs={{4,0},{0,4},{5,1},{1,5},{6,2},{2,6},{7,3},{3,7},{12,8},{8,12},{13,... | collective-permute-start | bytes 1290248 | tf_op jit(solution)/shard_map/ppermute | solution.py:18
  261.0 160.2 %collective-permute-start.4 = (bf16[2,28,6,640]{3,0,2,1:T(2,128)(2,1)}, bf16[2,28,6,640]{3,0,2,1:T(2,128)(2,1)}, u32[]{:S(2)}, u32[]{:S(2)}) collective-permute-start(bf16[2,28,6,640]{3,0,2,1:T(2,128)(2,1)} %copy.70), channel_id=1, source_target_pairs={{0,4},{4,0},{1,5},{5,1},{2,6},{6,2},{3,7},{7,3},{8,12},{12,8},{9,1... | collective-permute-start | bytes 1290248 | tf_op jit(solution)/shard_map/ppermute | solution.py:17
  262.4 0.6 copy-start.19
  262.4 0.6 copy-start.15
  262.4 0.6 copy-start.17
  419.7 2.6 copy-start.6
  419.7 2.6 copy-start.8
  422.3 0.7 copy-start.21
  422.9 8.4 %copy-start.16 = (s32[8,13]{1,0:T(8,128)S(1)}, s32[8,13]{1,0:T(8,128)}, u32[]{:S(2)}) copy-start(s32[8,13]{1,0:T(8,128)} %copy-done.15) | copy-start | bytes 1252
  422.9 8.4 %copy-start.18 = (s32[8,13]{1,0:T(8,128)S(1)}, s32[8,13]{1,0:T(8,128)}, u32[]{:S(2)}) copy-start(s32[8,13]{1,0:T(8,128)} %copy-done.17) | copy-start | bytes 1252
  422.9 8.5 %copy-start.20 = (pred[8,13]{1,0:T(8,128)(4,1)S(1)}, pred[8,13]{1,0:T(8,128)(4,1)}, u32[]{:S(2)}) copy-start(pred[8,13]{1,0:T(8,128)(4,1)} %copy-done.19) | copy-start | bytes 316
  425.3 41.5 %copy-start.22 = (pred[16]{0:T(512)(128)(4,1)S(1)}, pred[16]{0:T(512)(128)(4,1)}, u32[]{:S(2)}) copy-start(pred[16]{0:T(512)(128)(4,1)} %constant.225.clone.1) | copy-start | bytes 52
  425.3 41.3 %collective-permute-start.6 = (bf16[2,6,8,640]{3,2,1,0:T(8,128)(2,1)S(1)}, bf16[2,6,8,640]{3,2,1,0:T(8,128)(2,1)S(1)}, u32[]{:S(2)}, u32[]{:S(2)}) collective-permute-start(bf16[2,6,8,640]{3,2,1,0:T(8,128)(2,1)S(1)} %get-tuple-element.361), channel_id=1, source_target_pairs={{0,8},{8,16},{16,24},{1,9},{9,17},{17,25},{2,10},{10,18},{18,26},{... | collective-permute-start | bytes 368648 | tf_op jit(solution)/shard_map/ppermute | solution.py:17
  429.5 37.2 %collective-permute-start.7 = (bf16[2,6,8,640]{3,2,1,0:T(8,128)(2,1)S(1)}, bf16[2,6,8,640]{3,2,1,0:T(8,128)(2,1)S(1)}, u32[]{:S(2)}, u32[]{:S(2)}) collective-permute-start(bf16[2,6,8,640]{3,2,1,0:T(8,128)(2,1)S(1)} %get-tuple-element.362), channel_id=1, source_target_pairs={{8,0},{16,8},{24,16},{9,1},{17,9},{25,17},{10,2},{18,10},{26,18},{... | collective-permute-start | bytes 368648 | tf_op jit(solution)/shard_map/ppermute | solution.py:18
  466.6 1.0 copy-start.1
Sparse Core Ops, SparseCore 0:
  10.2 18.3 all-gather.2
  30.8 105.5 all-gather.4
  140.5 225.6 reduce-scatter.1
where the time goes:
time: 480 us; the launch traced here: 474 us
  local copies, waits for them, and re-layouts  226 us (47%)
  waiting for transfers between devices  107 us (22%)
  blocking collectives  34.3 us (7%)
  loops' own time  34.1 us (7%)
  other arithmetic  26.1 us (5%)
  matrix products  19.9 us (4%)
  between operations  14.2 us (3%)
  starting transfers between devices  12.3 us (3%)
    gather x3, local copies, waits for them, and re-layouts, local(): jnp.take_along_axis(table_core, col_take, axis=3)  156 us
    all_gather x1, waiting for transfers between devices, local(): lax.all_gather(w_out, ('lat', 'lon'), axis=0, tiled=True)  59.9 us
    psum x1, blocking collectives, local(): grad_table = lax.psum(table_local, ('lat', 'lon'))  34.3 us
    another operation x1, loops' own time, local(): lax.scan(block_step, (zero_pair, zero_table), jnp.arange(block_count, dty...  34.1 us
    all_gather x1, waiting for transfers between devices, local(): lax.all_gather(grad_out, 'chan', axis=2, tiled=True).reshape(tokens, -1)  18.7 us
    ppermute x4, waiting for transfers between devices, extended_2(): after = lax.ppermute(leading, axis, down)  14.7 us
    ppermute x4, waiting for transfers between devices, extended_2(): before = lax.ppermute(last, axis, up)  13 us
    dynamic_update_slice x4, other arithmetic, block_step(): lax.dynamic_update_slice_in_dim(grad_pair, prior_pair + new_part, key_loc...  12.3 us
  transfers between devices with their start and end apart: 11, of which 6 were waited for; matrix products, arithmetic and copies ran while one was open for 56% of the time, Pallas kernels for 0%

commit v1 on v0

v1 whole, which is shorter than its diff:
```python
import functools

import jax
import jax.numpy as jnp
from jax import lax
from jax.experimental import pallas as pl
from jax.experimental.pallas import tpu as pltpu
from jax.sharding import PartitionSpec as P

HEAD_DIM = 128
WIN = 13
REACH = WIN // 2
SCALE = HEAD_DIM ** (-0.5)
F32 = jnp.float32
BF16 = jnp.bfloat16


def row_slots(rows, cols):
    slots = max(rows + 2 * REACH, 2 * WIN - 1)
    while slots * cols % 128:
        slots += 1
    return slots


def column_pick(cols, slots):
    wide, tight = slots * 2 * cols, slots * cols
    source = lax.broadcasted_iota(jnp.int32, (wide, tight), 0)
    lane = lax.broadcasted_iota(jnp.int32, (wide, tight), 1)
    return (source == lane // cols * (2 * cols) + lane % cols).astype(F32)


def skew(value, cols, left):
    lanes = value.shape[1]
    place = lax.broadcasted_iota(jnp.int32, value.shape, 0) % cols
    step = 1
    while step < cols:
        moved = pltpu.roll(value, lanes - step if left else step, 1)
        value = jnp.where(place // step % 2 == 1, moved, value)
        step *= 2
    return value


def expand_bias(diag, cols, slots):
    lanes = diag.shape[1]
    rows = [jnp.broadcast_to(diag[i : i + 1], (cols, lanes)) for i in range(diag.shape[0])]
    wide = pltpu.roll(jnp.concatenate(rows, axis=0), lanes - (cols - 1), 1)
    wide = skew(wide, cols, False)
    return jnp.dot(
        wide, column_pick(cols, slots), precision=lax.Precision.HIGHEST, preferred_element_type=F32
    )


def collapse_bias(spread, cols, slots):
    wide = lax.dot_general(
        spread,
        column_pick(cols, slots),
        (((1,), (1,)), ((), ())),
        precision=lax.Precision.HIGHEST,
        preferred_element_type=F32,
    )
    wide = skew(pltpu.roll(wide, cols - 1, 1), cols, True)
    return jnp.sum(wide.reshape(-1, cols, wide.shape[1]), axis=1)


def allowed_pairs(valid, lat_first, lat_total, rows, cols, slots, blocks, lon_size):
    shape = (rows * cols, blocks * slots * cols)
    query = lax.broadcasted_iota(jnp.int32, shape, 0)
    lane = lax.broadcasted_iota(jnp.int32, shape, 1)
    block = lane // (slots * cols)
    key = lane % (slots * cols)
    row = lat_first + query // cols
    first = jnp.clip(row - REACH, 0, lat_total - WIN)
    key_row = lat_first - REACH + key // cols
    delta = key % cols - query % cols
    in_lat = (key_row >= first) & (key_row < first + WIN)
    near = (delta >= -REACH) & (delta <= REACH)
    right = delta + cols <= REACH
    left = delta - cols >= -REACH
    if blocks == 1:
        in_lon = near
    elif lon_size == 2:
        in_lon = ((block == 0) & near) | ((block == 1) & (right | left))
    else:
        in_lon = ((block == 0) & near) | ((block == 1) & right) | ((block == 2) & left)
    return in_lat & in_lon & (valid > 0)


def attend(dims, allowed, spread, q, g, k, v):
    rows, cols, slots, blocks = dims
    span = slots * cols
    nt = (((1,), (1,)), ((), ()))
    tn = (((0,), (0,)), ((), ()))
    shifts = [((i - REACH) * cols) % span for i in range(rows)]
    bias = jnp.concatenate(
        [
            jnp.concatenate([pltpu.roll(part, s, 1) if s else part for s in shifts], axis=0)
            for part in (spread[b * cols : (b + 1) * cols] for b in range(blocks))
        ],
        axis=1,
    )
    scores = SCALE * lax.dot_general(q, k, nt, preferred_element_type=F32) + bias
    scores = jnp.where(allowed, scores, -1e30)
    weights = jnp.exp(scores - jnp.max(scores, axis=1, keepdims=True))
    probs = weights / jnp.sum(weights, axis=1, keepdims=True)
    grad_prob = lax.dot_general(g, v, nt, preferred_element_type=F32)
    grad_prob = jnp.where(allowed, grad_prob, 0.0)
    delta = jnp.sum(probs * grad_prob, axis=1, keepdims=True)
    dscore = probs * (grad_prob - delta)
    folded = []
    for b in range(blocks):
        total = None
        for i, s in enumerate(shifts):
            part = dscore[i * cols : (i + 1) * cols, b * span : (b + 1) * span]
            part = pltpu.roll(part, (span - s) % span, 1) if s else part
            total = part if total is None else total + part
        folded.append(total)
    low = dscore.astype(BF16)
    prob_low = probs.astype(BF16)
    grad_q = SCALE * jnp.dot(low, k, preferred_element_type=F32)
    grad_k = SCALE * lax.dot_general(low, q, tn, preferred_element_type=F32)
    grad_v = lax.dot_general(prob_low, g, tn, preferred_element_type=F32)
    return grad_q, grad_k, grad_v, folded


def attention_kernel(dims, lon_size, lat_size, valid, diag, q, g, kv, gq, gkv, table, pairs, fold):
    rows, cols, slots, blocks = dims
    lat_first = lax.axis_index("lat") * rows
    heads = q.shape[1] // HEAD_DIM
    allowed = allowed_pairs(
        valid[...], lat_first, lat_size * rows, rows, cols, slots, blocks, lon_size
    )
    spread = expand_bias(diag[...], cols, slots)
    for h in range(heads):
        at = pl.ds(h * HEAD_DIM, HEAD_DIM)
        own = spread[h * blocks * cols : (h + 1) * blocks * cols]
        grad_q, grad_k, grad_v, folded = attend(
            dims, allowed, own, q[:, at], g[:, at], kv[0, :, at], kv[1, :, at]
        )
        gq[:, at] = grad_q.astype(BF16)
        gkv[0, :, at] = grad_k
        gkv[1, :, at] = grad_v
        for b in range(blocks):
            fold[pl.ds((h * blocks + b) * cols, cols), :] = folded[b]
    table[...] = collapse_bias(fold[...], cols, slots)


def diag_table(table, cols, slots, blocks, lon_size):
    heads, height, width = table.shape

    def placed(part, first):
        return jnp.pad(part, ((0, 0), (0, 0), (first, 2 * cols - first - part.shape[2])))

    own = placed(table, cols - 1 - REACH)
    right = placed(table[:, :, REACH + 1 :], 0) if blocks > 1 else None
    left = placed(table[:, :, :REACH], 2 * cols - 1 - REACH) if blocks > 1 else None
    parts = [own] if blocks == 1 else [own, right + left] if lon_size == 2 else [own, right, left]
    stacked = jnp.stack(parts, axis=1)
    stacked = jnp.pad(stacked, ((0, 0), (0, 0), (0, slots - height), (0, 0)))
    return stacked.reshape(heads * blocks, slots * 2 * cols)


def undiag_table(diag, heads, cols, slots, blocks, lon_size):
    grid = diag.reshape(heads, blocks, slots, 2 * cols)[:, :, : 2 * WIN - 1]
    first = cols - 1 - REACH
    own = grid[:, 0, :, first : first + WIN]
    if blocks == 1:
        return own
    right = grid[:, 1, :, :REACH]
    left = grid[:, blocks - 1, :, 2 * cols - 1 - REACH : 2 * cols - 1]
    gap = jnp.zeros(own.shape[:2] + (1,), own.dtype)
    return own + jnp.concatenate([left, gap, right], axis=2)


def valid_row(key_mask, rows, cols, slots, blocks, lon_size):
    lat_total, lon_total = key_mask.shape
    mark = (jnp.arange(lat_total) % 4 == 0)[:, None] & (jnp.arange(lon_total) % 4 == 0)[None, :]
    valid = ((key_mask == 1) | mark).astype(jnp.int32)
    valid = jnp.pad(valid, ((REACH, slots), (0, 0)))
    valid = lax.dynamic_slice_in_dim(valid, lax.axis_index("lat") * rows, slots, 0)
    me = lax.axis_index("lon")
    parts = [
        lax.dynamic_slice_in_dim(valid, (me + step) % lon_size * cols, cols, 1)
        for step in (0, 1, lon_size - 1)[:blocks]
    ]
    return jnp.stack(parts, axis=0).reshape(1, blocks * slots * cols)


def local(queries, keys, values, attn_out, grad_out, w_out, bias_table, key_mask):
    rows, cols, width = queries.shape
    heads = bias_table.shape[0]
    tokens = rows * cols
    lat_size, lon_size = lax.axis_size("lat"), lax.axis_size("lon")
    blocks = min(3, lon_size)
    slots = row_slots(rows, cols)
    span = slots * cols
    rim = REACH * cols
    group = ("lat", "lon")
    dims = (rows, cols, slots, blocks)
    whole = lax.all_gather(grad_out.reshape(tokens, -1), "chan", axis=1, tiled=True)
    features = lax.all_to_all(whole, group, split_axis=1, concat_axis=0, tiled=True)
    part = jnp.dot(features, w_out, preferred_element_type=F32).astype(BF16)
    back = lax.all_to_all(part, group, split_axis=0, concat_axis=0, tiled=True)
    grad_attn = jnp.sum(back.reshape(-1, tokens, width).astype(F32), axis=0).astype(BF16)

    kv = jnp.stack([keys, values]).reshape(2, 1, tokens, width)
    rights = [(i, (i + 1) % lon_size) for i in range(lon_size)]
    lefts = [(j, i) for i, j in rights]
    sides = [kv]
    if blocks > 1:
        sides.append(lax.ppermute(kv, "lon", lefts))
    if blocks > 2:
        sides.append(lax.ppermute(kv, "lon", rights))
    kv = jnp.concatenate(sides, axis=1)
    up = [(i, i + 1) for i in range(lat_size - 1)]
    down = [(j, i) for i, j in up]
    before = lax.ppermute(kv[:, :, tokens - rim :], "lat", up)
    after = lax.ppermute(kv[:, :, :rim], "lat", down)
    pad = jnp.zeros((2, blocks, span - tokens - 2 * rim, width), BF16)
    kv = jnp.concatenate([before, kv, after, pad], axis=2).reshape(2, blocks * span, width)

    diag = diag_table(bias_table, cols, slots, blocks, lon_size)
    valid = valid_row(key_mask, rows, cols, slots, blocks, lon_size)
    vmem = pl.BlockSpec(memory_space=pltpu.VMEM)
    grad_queries, grad_kv, diag_grad = pl.pallas_call(
        functools.partial(attention_kernel, dims, lon_size, lat_size),
        out_shape=(
            jax.ShapeDtypeStruct((tokens, width), BF16),
            jax.ShapeDtypeStruct((2, blocks * span, width), F32),
            jax.ShapeDtypeStruct((heads * blocks, slots * 2 * cols), F32),
        ),
        in_specs=[vmem] * 5,
        out_specs=(vmem,) * 3,
        scratch_shapes=[
            pltpu.VMEM((8, 128), F32),
            pltpu.VMEM((heads * blocks * cols, span), F32),
        ],
        compiler_params=pltpu.CompilerParams(vmem_limit_bytes=40 * 1024 * 1024),
    )(valid, diag, queries.reshape(tokens, width), grad_attn, kv)

    grad_kv = grad_kv.reshape(2, blocks, span, width)
    own_before = lax.ppermute(grad_kv[:, :, :rim].astype(BF16), "lat", down).astype(F32)
    own_after = lax.ppermute(
        grad_kv[:, :, rim + tokens : 2 * rim + tokens].astype(BF16), "lat", up
    ).astype(F32)
    middle = grad_kv[:, :, rim : rim + tokens]
    middle = (
        middle
        + jnp.pad(own_before, ((0, 0), (0, 0), (tokens - rim, 0), (0, 0)))
        + jnp.pad(own_after, ((0, 0), (0, 0), (0, tokens - rim), (0, 0)))
    )
    total = middle[:, 0]
    if blocks > 1:
        total = total + lax.ppermute(middle[:, 1].astype(BF16), "lon", rights).astype(F32)
    if blocks > 2:
        total = total + lax.ppermute(middle[:, 2].astype(BF16), "lon", lefts).astype(F32)
    total = total.astype(BF16).reshape(2, rows, cols, width)
    diag_grad = lax.psum(diag_grad, group)
    grad_table = undiag_table(diag_grad, heads, cols, slots, blocks, lon_size)
    saved = lax.all_gather(attn_out.reshape(tokens, width), group, axis=0, tiled=True)
    grad_wout = lax.dot_general(
        features, saved, (((0,), (0,)), ((), ())), preferred_element_type=F32
    )
    return (grad_queries.reshape(rows, cols, width), total[0], total[1], grad_wout, grad_table)


def solution(mesh):
    token = P("lat", "lon", "chan")
    matrix = P(("lat", "lon"), "chan")
    table = P("chan", None, None)
    return jax.shard_map(
        local,
        mesh=mesh,
        in_specs=(token, token, token, token, token, matrix, table, P()),
        out_specs=(token, token, token, matrix, table),
        check_vma=False,
    )
```

time: 480 us -> 204 us (0.42)
  the two profiles are of different devices: /device:TPU:12 before, /device:TPU:0 now
where the time goes in v1:
time: 204 us
  blocking collectives  75 us (37%)
  waiting for transfers between devices  58.2 us (29%)
  starting transfers between devices  24.8 us (12%)
  between operations  15.7 us (8%)
  local copies, waits for them, and re-layouts  10.6 us (5%)
  other arithmetic  7.96 us (4%)
  matrix products  6.47 us (3%)
  Pallas kernels  4.95 us (2%)
    psum x1, blocking collectives, local(): diag_grad = lax.psum(diag_grad, group)  38 us
    all_to_all x1, blocking collectives, local(): lax.all_to_all(whole, group, split_axis=1, concat_axis=0, tiled=True)  37 us
    all_gather x1, waiting for transfers between devices, local(): lax.all_gather(grad_out.reshape(tokens, -1), 'chan', axis=1, tiled=True)  22.6 us
    ppermute x1, waiting for transfers between devices, local(): sides.append(lax.ppermute(kv, 'lon', lefts))  19.8 us
    ppermute x1, starting transfers between devices, local(): lax.ppermute(grad_kv[:, :, rim + tokens:2 * rim + tokens].astype(BF16), '...  11 us
    ppermute x1, waiting for transfers between devices, local(): after = lax.ppermute(kv[:, :, :rim], 'lat', down)  8.52 us
    ppermute x1, waiting for transfers between devices, local(): lax.ppermute(middle[:, 1].astype(BF16), 'lon', rights).astype(F32)  6.12 us
    ppermute x1, starting transfers between devices, local(): before = lax.ppermute(kv[:, :, tokens - rim:], 'lat', up)  5.27 us
  transfers between devices with their start and end apart: 9, of which 4 were waited for; matrix products, arithmetic and copies ran while one was open for 6% of the time, Pallas kernels for 2%

profile of v1, /device:TPU:0, one launch (start us, length us, event | category | flops | bytes accessed | tf_op | source)
XLA Modules:
  0.0 203.7 jit_solution(4413673531353038375)
XLA Ops:
  8.0 0.0 copy-start
  8.0 0.0 all-gather.3.cloned.1.call-start
  8.1 0.7 all-gather.3.cloned.1.call-update
  8.7 22.6 %all-gather.3.cloned.1.call-done = bf16[128,5120]{1,0:T(8,128)(2,1)} async-done(((bf16[128,1280]{1,0:T(8,128)(2,1)}), bf16[128,5120]{1,0:T(8,128)(2,1)}) %all-gather.3.cloned.1.call-update) | async-done | bytes 1310736 | tf_op jit(solution)/shard_map/all_gather | solution.py:199
  31.3 1.8 copy.32
  33.1 37.0 %all_to_all.28 = bf16[128,8,640]{0,2,1:T(8,128)(2,1)S(1)} all-to-all(bf16[128,8,640]{0,2,1:T(8,128)(2,1)S(1)} %bitcast.57), channel_id=1, replica_groups=mesh['lat'=4,'lon'=2,'chan'=4] {'lat','lon'}, dimensions={1} | all-to-all | bytes 2621440 | tf_op jit(solution)/shard_map/all_to_all | solution.py:200
  70.2 0.7 copy.33
  70.9 0.0 copy-start.6
  70.9 0.0 copy-done
  70.9 2.4 %convolution_convert_fusion = bf16[1024,640]{1,0:T(8,128)(2,1)} fusion(bf16[1024,640]{1,0:T(8,128)(2,1)S(1)} %bitcast.65, bf16[640,640]{1,0:T(8,128)(2,1)S(1)} %copy-done), kind=kOutput, calls=%fused_computation | convolution fusion | flops 839516160 | bytes 3440640 | tf_op jit(solution)/shard_map/dot_general | solution.py:201
  73.3 0.0 copy-start.4
  73.3 0.0 copy-start.5
  73.3 0.0 copy-start.9
  73.3 0.0 copy-done.6
  73.3 3.8 %all-to-all-start.1 = ((bf16[8,128,640]{2,1,0:T(8,128)(2,1)}), bf16[8,128,640]{2,1,0:T(8,128)(2,1)S(1)}, u32[]{:S(2)}, u32[]{:S(2)}) async-start(bf16[8,128,640]{2,1,0:T(8,128)(2,1)} %bitcast.67), calls=%async_computation.1 | async-start | bytes 2621440 | tf_op jit(solution)/shard_map/all_to_all | solution.py:202
  77.1 0.0 all-gather.5.cloned.1.call-start
  77.1 0.5 all-gather.5.cloned.1.call-update
  77.6 0.0 copy-done.4
  77.6 0.0 copy-done.5
  77.7 2.1 %collective-permute-start = (bf16[2,1,128,640]{3,2,1,0:T(8,128)(2,1)S(1)}, bf16[2,1,128,640]{3,2,1,0:T(8,128)(2,1)S(1)}, u32[]{:S(2)}, u32[]{:S(2)}) collective-permute-start(bf16[2,1,128,640]{3,2,1,0:T(8,128)(2,1)S(1)} %pad_maximum_fusion), channel_id=1, source_target_pairs={{4,0},{0,4},{5,1},{1,5},{6,2},{2,6},{7,3},{3,7},{12,8},{8,12},{13,... | collective-permute-start | bytes 983048 | tf_op jit(solution)/shard_map/ppermute | solution.py:210
  79.8 0.0 copy-done.9
  79.8 0.1 and_or_fusion
  79.9 0.1 pad_convert_fusion
  80.0 0.1 dynamic-slice_bitcast_fusion.1
  80.0 0.0 copy-done.8
  80.0 19.8 %collective-permute-done = bf16[2,1,128,640]{3,2,1,0:T(8,128)(2,1)S(1)} collective-permute-done((bf16[2,1,128,640]{3,2,1,0:T(8,128)(2,1)S(1)}, bf16[2,1,128,640]{3,2,1,0:T(8,128)(2,1)S(1)}, u32[]{:S(2)}, u32[]{:S(2)}) %collective-permute-start) | collective-permute-done | bytes 327712 | tf_op jit(solution)/shard_map/ppermute | solution.py:210
  99.8 0.7 pad_maximum_fusion.3
  100.6 1.3 collective-permute-start.2
  101.8 5.3 %collective-permute-start.1 = (bf16[2,2,48,640]{3,2,1,0:T(8,128)(2,1)S(1)}, bf16[2,2,48,640]{3,2,1,0:T(8,128)(2,1)}, u32[]{:S(2)}, u32[]{:S(2)}) collective-permute-start(bf16[2,2,48,640]{3,2,1,0:T(8,128)(2,1)S(1)} %get-tuple-element.28), channel_id=1, source_target_pairs={{0,8},{8,16},{16,24},{1,9},{9,17},{17,25},{2,10},{10,18},{18,26},{... | collective-permute-start | bytes 737288 | tf_op jit(solution)/shard_map/ppermute | solution.py:216
  107.1 0.1 copy.30
  107.2 0.1 reshape.75.valid
  107.3 0.1 copy.41
  107.5 0.1 reshape.76.diag
  107.6 0.1 pad.55.clone
  107.7 0.1 pad.48.clone
  107.8 8.5 %collective-permute-done.2 = bf16[2,2,48,640]{3,2,1,0:T(8,128)(2,1)} collective-permute-done((bf16[2,2,48,640]{3,2,1,0:T(8,128)(2,1)}, bf16[2,2,48,640]{3,2,1,0:T(8,128)(2,1)}, u32[]{:S(2)}, u32[]{:S(2)}) %collective-permute-start.2) | collective-permute-done | bytes 245792 | tf_op jit(solution)/shard_map/ppermute | solution.py:217
  116.3 0.0 collective-permute-done.1
  116.3 2.4 %maximum_maximum_fusion = bf16[2,2,256,640]{3,2,1,0:T(8,128)(2,1)} fusion(bf16[2,2,48,640]{3,2,1,0:T(8,128)(2,1)} %collective-permute-done.2, bf16[2,1,128,640]{3,2,1,0:T(8,128)(2,1)S(1)} %collective-permute-done, bf16[1,1,128,640]{3,2,1,0:T(8,128)(2,1)S(1)} %bitcast.61, bf16[1,1,128,640]{3,2,1,0:T(8,128)(2,1)S(1)} %bitcast.64, ...), kind=kLoop, calls=%fused_computation.3 | loop fusion | flops 7864320 | bytes 2458112 | tf_op jit(solution)/shard_map/concatenate | solution.py:219
  118.7 0.0 all-to-all-done.1
  118.7 0.9 reduce_sum.12.g
  119.6 1.3 copy-done.1
  120.9 0.9 copy-done.2
  121.8 0.9 copy-done.3
  122.8 4.9 %shard_map.119 = (bf16[128,640]{1,0:T(8,128)(2,1)}, f32[2,512,640]{2,1,0:T(8,128)S(1)}, f32[10,512]{1,0:T(8,128)S(1)}) custom-call(s32[1,512]{1,0:T(1,128)S(1)} %reshape.75.valid, f32[10,512]{1,0:T(8,128)S(1)} %reshape.76.diag, bf16[128,640]{1,0:T(8,128)(2,1)S(1)} %bitcast.56, bf16[128,640]{1,0:T(8,128)(2,1)S(1)} %copy-done.2, bf16[2,512,640]{2,1,0:T(8,128)(2,1)S(1)} %bitcast.55), custom_call_target="tpu_custom_call" | custom-call | tf_op jit(solution)/shard_map/pallas_call | solution.py:224
  127.7 0.1 convert.14
  127.9 0.8 fusion.7
  128.7 11.0 %collective-permute-start.4 = (bf16[2,2,48,640]{3,2,1,0:T(8,128)(2,1)}, bf16[2,2,48,640]{3,2,1,0:T(8,128)(2,1)}, u32[]{:S(2)}, u32[]{:S(2)}) collective-permute-start(bf16[2,2,48,640]{3,2,1,0:T(8,128)(2,1)} %get-tuple-element.27), channel_id=1, source_target_pairs={{0,8},{8,16},{16,24},{1,9},{9,17},{17,25},{2,10},{10,18},{18,26},{... | collective-permute-start | bytes 737288 | tf_op jit(solution)/shard_map/ppermute | solution.py:242
  139.7 1.3 collective-permute-start.3
  140.9 0.0 all-gather.5.cloned.1.call-done
  141.0 4.1 %fusion.9 = f32[640,640]{1,0:T(8,128)} fusion(bf16[1024,640]{1,0:T(8,128)(2,1)} %bitcast.66, bf16[1024,640]{1,0:T(8,128)(2,1)} %all-gather.5.cloned.1.call-done), kind=kOutput, calls=%fused_computation.33 | convolution fusion | flops 838860800 | bytes 4259840 | tf_op jit(solution)/shard_map/dot_general | solution.py:260
  145.1 0.8 reshape.83
  145.9 38.0 %psum.7 = f32[5,2,32,16]{3,2,1,0:T(8,128)} all-reduce(f32[5,2,32,16]{3,2,1,0:T(8,128)} %reshape.83), channel_id=1, replica_groups=mesh['lat'=4,'lon'=2,'chan'=4] {'lat','lon'}, use_global_device_ids=true, to_apply=%region_1.2 | all-reduce | flops 5120 | bytes 40960 | tf_op jit(solution)/shard_map/psum | solution.py:257
  183.8 0.0 collective-permute-done.4
  183.8 0.0 collective-permute-done.3
  183.9 2.3 %fusion = f32[2,2,128,640]{3,2,1,0:T(8,128)} fusion(f32[2,2,256,640]{3,2,1,0:T(8,128)S(1)} %bitcast.54, bf16[2,2,48,640]{3,2,1,0:T(8,128)(2,1)} %collective-permute-done.4, bf16[2,2,48,640]{3,2,1,0:T(8,128)(2,1)} %collective-permute-done.3), kind=kLoop, calls=%fused_computation.2 | loop fusion | flops 1310720 | bytes 3112960 | tf_op jit(solution)/shard_map/add | solution.py:247
  186.1 1.1 fusion.3
  187.3 0.1 collective-permute-start.5
  187.3 0.0 copy-done.7
  187.4 0.1 slice_bitcast_fusion.4
  187.4 0.1 fusion.4
  187.6 0.7 copy.37
  188.3 6.1 %collective-permute-done.5 = bf16[2,128,640]{2,1,0:T(8,128)(2,1)S(1)} collective-permute-done((bf16[2,128,640]{2,1,0:T(8,128)(2,1)S(1)}, bf16[2,128,640]{2,1,0:T(8,128)(2,1)S(1)}, u32[]{:S(2)}, u32[]{:S(2)}) %collective-permute-start.5) | collective-permute-done | bytes 327712 | tf_op jit(solution)/shard_map/ppermute | solution.py:253
  194.4 1.1 fusion.2
  195.6 0.8 slice_bitcast_fusion.1
  (14 shorter events, 0.1 us)
Async XLA Ops:
  8.0 62.9 %copy-start = (bf16[640,640]{1,0:T(8,128)(2,1)S(1)}, bf16[640,640]{1,0:T(8,128)(2,1)}, u32[]{:S(2)}) copy-start(bf16[640,640]{1,0:T(8,128)(2,1)} %param.13) | copy-start | bytes 2457604
  8.0 23.3 %all-gather.3.cloned.1.call-start = ((), (), s32[]{:S(2)}) async-start(), calls=%async_computation.2 | async-start | bytes 1638400 | tf_op jit(solution)/shard_map/all_gather | solution.py:199
  70.9 2.4 %copy-start.6 = (bf16[8,128,640]{2,1,0:T(8,128)(2,1)}, bf16[8,128,640]{2,1,0:T(8,128)(2,1)S(1)}, u32[]{:S(2)}) copy-start(bf16[8,128,640]{2,1,0:T(8,128)(2,1)S(1)} %copy.33) | copy-start | bytes 3932164
  73.3 4.4 %copy-start.4 = (bf16[16,8,640]{2,1,0:T(8,128)(2,1)S(1)}, bf16[16,8,640]{2,1,0:T(8,128)(2,1)}, u32[]{:S(2)}) copy-start(bf16[16,8,640]{2,1,0:T(8,128)(2,1)} %param.10) | copy-start | bytes 491524
  73.3 4.4 %copy-start.5 = (bf16[16,8,640]{2,1,0:T(8,128)(2,1)S(1)}, bf16[16,8,640]{2,1,0:T(8,128)(2,1)}, u32[]{:S(2)}) copy-start(bf16[16,8,640]{2,1,0:T(8,128)(2,1)} %param.9) | copy-start | bytes 491524
  73.3 6.5 %copy-start.9 = (s32[64,16]{0,1:T(8,128)S(1)}, s32[64,16]{0,1:T(8,128)}, u32[]{:S(2)}) copy-start(s32[64,16]{0,1:T(8,128)} %param.15) | copy-start | bytes 12292
  73.3 6.8 %copy-start.8 = (f32[5,25,13]{1,2,0:T(8,128)S(1)}, f32[5,25,13]{1,2,0:T(8,128)}, u32[]{:S(2)}) copy-start(f32[5,25,13]{1,2,0:T(8,128)} %param.14) | copy-start | bytes 19504
  73.3 45.5 %all-to-all-start.1 = ((bf16[8,128,640]{2,1,0:T(8,128)(2,1)}), bf16[8,128,640]{2,1,0:T(8,128)(2,1)S(1)}, u32[]{:S(2)}, u32[]{:S(2)}) async-start(bf16[8,128,640]{2,1,0:T(8,128)(2,1)} %bitcast.67), calls=%async_computation.1 | async-start | bytes 2621440 | tf_op jit(solution)/shard_map/all_to_all | solution.py:202
  77.1 63.9 %all-gather.5.cloned.1.call-start = ((), (), s32[]{:S(2)}) async-start(), calls=%async_computation.3 | async-start | bytes 1474560 | tf_op jit(solution)/shard_map/all_gather | solution.py:259
  77.7 22.1 %collective-permute-start = (bf16[2,1,128,640]{3,2,1,0:T(8,128)(2,1)S(1)}, bf16[2,1,128,640]{3,2,1,0:T(8,128)(2,1)S(1)}, u32[]{:S(2)}, u32[]{:S(2)}) collective-permute-start(bf16[2,1,128,640]{3,2,1,0:T(8,128)(2,1)S(1)} %pad_maximum_fusion), channel_id=1, source_target_pairs={{4,0},{0,4},{5,1},{1,5},{6,2},{2,6},{7,3},{3,7},{12,8},{8,12},{13,... | collective-permute-start | bytes 983048 | tf_op jit(solution)/shard_map/ppermute | solution.py:210
  100.6 15.7 %collective-permute-start.2 = (bf16[2,2,48,640]{3,2,1,0:T(8,128)(2,1)}, bf16[2,2,48,640]{3,2,1,0:T(8,128)(2,1)}, u32[]{:S(2)}, u32[]{:S(2)}) collective-permute-start(bf16[2,2,48,640]{3,2,1,0:T(8,128)(2,1)} %get-tuple-element.29), channel_id=1, source_target_pairs={{8,0},{16,8},{24,16},{9,1},{17,9},{25,17},{10,2},{18,10},{26,18},{... | collective-permute-start | bytes 737288 | tf_op jit(solution)/shard_map/ppermute | solution.py:217
  101.8 14.5 %collective-permute-start.1 = (bf16[2,2,48,640]{3,2,1,0:T(8,128)(2,1)S(1)}, bf16[2,2,48,640]{3,2,1,0:T(8,128)(2,1)}, u32[]{:S(2)}, u32[]{:S(2)}) collective-permute-start(bf16[2,2,48,640]{3,2,1,0:T(8,128)(2,1)S(1)} %get-tuple-element.28), channel_id=1, source_target_pairs={{0,8},{8,16},{16,24},{1,9},{9,17},{17,25},{2,10},{10,18},{18,26},{... | collective-permute-start | bytes 737288 | tf_op jit(solution)/shard_map/ppermute | solution.py:216
  119.6 1.3 copy-start.1
  120.9 0.9 copy-start.2
  121.8 0.9 copy-start.3
  128.7 55.2 %collective-permute-start.4 = (bf16[2,2,48,640]{3,2,1,0:T(8,128)(2,1)}, bf16[2,2,48,640]{3,2,1,0:T(8,128)(2,1)}, u32[]{:S(2)}, u32[]{:S(2)}) collective-permute-start(bf16[2,2,48,640]{3,2,1,0:T(8,128)(2,1)} %get-tuple-element.27), channel_id=1, source_target_pairs={{0,8},{8,16},{16,24},{1,9},{9,17},{17,25},{2,10},{10,18},{18,26},{... | collective-permute-start | bytes 737288 | tf_op jit(solution)/shard_map/ppermute | solution.py:242
  139.7 44.2 %collective-permute-start.3 = (bf16[2,2,48,640]{3,2,1,0:T(8,128)(2,1)}, bf16[2,2,48,640]{3,2,1,0:T(8,128)(2,1)}, u32[]{:S(2)}, u32[]{:S(2)}) collective-permute-start(bf16[2,2,48,640]{3,2,1,0:T(8,128)(2,1)} %get-tuple-element.26), channel_id=1, source_target_pairs={{8,0},{16,8},{24,16},{9,1},{17,9},{25,17},{10,2},{18,10},{26,18},{... | collective-permute-start | bytes 737288 | tf_op jit(solution)/shard_map/ppermute | solution.py:241
  183.8 3.5 %copy-start.7 = (f32[5,2,32,16]{3,2,1,0:T(8,128)S(1)}, f32[5,2,32,16]{3,2,1,0:T(8,128)}, u32[]{:S(2)}) copy-start(f32[5,2,32,16]{3,2,1,0:T(8,128)} %psum.7) | copy-start | bytes 61444
  187.3 7.1 %collective-permute-start.5 = (bf16[2,128,640]{2,1,0:T(8,128)(2,1)S(1)}, bf16[2,128,640]{2,1,0:T(8,128)(2,1)S(1)}, u32[]{:S(2)}, u32[]{:S(2)}) collective-permute-start(bf16[2,128,640]{2,1,0:T(8,128)(2,1)S(1)} %fusion.3), channel_id=1, source_target_pairs={{0,4},{4,0},{1,5},{5,1},{2,6},{6,2},{3,7},{7,3},{8,12},{12,8},{9,1... | collective-permute-start | bytes 983048 | tf_op jit(solution)/shard_map/ppermute | solution.py:253
Sparse Core Ops, SparseCore 0:
  10.4 20.8 all-gather.2
Sparse Core Ops, SparseCore 1:
  79.7 51.3 all-gather.4

commit v2 on v1

--- a/solution.py
+++ b/solution.py
@@ -122,26 +122,329 @@
     return grad_q, grad_k, grad_v, folded
 
 
-def attention_kernel(dims, lon_size, lat_size, valid, diag, q, g, kv, gq, gkv, table, pairs, fold):
+def mega_kernel(
+    dims,
+    sizes,
+    valid,
+    diag,
+    q,
+    keys,
+    values,
+    grad_out,
+    w_out,
+    gq,
+    gk,
+    gv,
+    table,
+    features,
+    kv,
+    feat,
+    part,
+    back,
+    grad_attn,
+    gkv,
+    gsend,
+    gmid,
+    grim,
+    fold,
+    tables,
+    feat_out_sem,
+    feat_sem,
+    pass_sem,
+    part_out_sem,
+    part_sem,
+    kv_out_sem,
+    kv_sem,
+    g_out_sem,
+    g_sem,
+    t_out_sem,
+    t_sem,
+    own_sem,
+):
     rows, cols, slots, blocks = dims
-    lat_first = lax.axis_index("lat") * rows
-    heads = q.shape[1] // HEAD_DIM
+    lat_size, lon_size, chan_size = sizes
+    tokens, width = q.shape
+    heads = width // HEAD_DIM
+    span, rim = slots * cols, REACH * cols
+    depth = w_out.shape[0]
+    slices = grad_out.shape[0]
+    group = lat_size * lon_size
+    lat, lon, chan = lax.axis_index("lat"), lax.axis_index("lon"), lax.axis_index("chan")
+    me = lat * lon_size + lon
+    source_chan = me // slices
+    mesh_id = pl.DeviceIdType.MESH
+
+    def remote(src, dst, send, recv, where):
+        return pltpu.make_async_remote_copy(
+            src_ref=src,
+            dst_ref=dst,
+            send_sem=send,
+            recv_sem=recv,
+            device_id=where,
+            device_id_type=mesh_id,
+        )
+
+    def place(index):
+        return index // lon_size, lax.rem(index, lon_size)
+
+    total_devices = group * chan_size
+    mine = me * chan_size + chan
+    barrier = pltpu.get_barrier_semaphore()
+
+    def greet(step, carry):
+        other = lax.rem(mine + step, total_devices)
+        to_lat, to_lon = place(other // chan_size)
+        pl.semaphore_signal(
+            barrier,
+            inc=1,
+            device_id=(to_lat, to_lon, lax.rem(other, chan_size)),
+            device_id_type=mesh_id,
+        )
+        return carry
+
+    lax.fori_loop(1, total_devices, greet, 0)
+    own_copies = [
+        pltpu.make_async_copy(x, kv.at[i, 0, pl.ds(rim, tokens)], own_sem.at[i])
+        for i, x in enumerate((keys, values))
+    ]
+    for copy in own_copies:
+        copy.start()
+    pl.semaphore_wait(barrier, total_devices - 1)
+
+    def block_at(index):
+        return pl.ds(pl.multiple_of(index * tokens, tokens), tokens)
+
+    def feature_copy(i, j):
+        target = chan * slices + i
+        to_lat, to_lon = place(target)
+        to_chan = 2 * j + lax.rem(chan, 2)
+        away = (target != me) | (to_chan != chan)
+        src, dst = grad_out.at[i], feat.at[block_at(me)]
+        out = remote(
+            src, dst, feat_out_sem.at[i, j], feat_sem.at[me], (to_lat, to_lon, to_chan)
+        )
+        return away, out, pltpu.make_async_copy(src, dst, feat_sem.at[me])
+
+    for i in range(slices):
+        for j in range(chan_size // 2):
+            away, out, own = feature_copy(i, j)
+            pl.when(away)(out.start)
+            pl.when(jnp.logical_not(away))(own.start)
+
+    def rim_pieces():
+        pieces = []
+        for b in range(blocks):
+            to_lon = lax.rem(lon + (0, lon_size - 1, 1)[b], lon_size)
+            from_lon = lax.rem(lon + (0, 1, lon_size - 1)[b], lon_size)
+            for d, (shift, own, ext) in enumerate(
+                (
+                    (0, (0, tokens), (rim, tokens)),
+                    (1, (tokens - rim, rim), (0, rim)),
+                    (-1, (0, rim), (rim + tokens, rim)),
+                )
+            ):
+                if b or d:
+                    pieces.append((b, d, shift, own, ext, to_lon, from_lon))
+        return pieces
+
+    def inside(shift):
+        return (lat + shift >= 0) & (lat + shift < lat_size)
+
+    def kv_copy(piece, i):
+        b, d, shift, own, ext, to_lon, _ = piece
+        return remote(
+            (keys, values)[i].at[pl.ds(*own)],
+            kv.at[i, b, pl.ds(*ext)],
+            kv_out_sem.at[i, b, d],
+            kv_sem.at[i, b, d],
+            (lat + shift, to_lon, chan),
+        )
+
+    for piece in rim_pieces():
+        for i in range(2):
+            pl.when(inside(piece[2]))(kv_copy(piece, i).start)
+
+    last = 2 * rim + tokens
+    for i in range(2):
+        for b in range(blocks):
+            if span > last:
+                kv[i, b, pl.ds(last, span - last), :] = jnp.zeros((span - last, width), BF16)
+
+            @pl.when(lat == 0)
+            def _():
+                kv[i, b, pl.ds(0, rim), :] = jnp.zeros((rim, width), BF16)
+
+            @pl.when(lat == lat_size - 1)
+            def _():
+                kv[i, b, pl.ds(rim + tokens, rim), :] = jnp.zeros((rim, width), BF16)
+
+    lat_first = lat * rows
+    primary = lax.rem(source_chan, 2) == lax.rem(chan, 2)
+
+    def pass_copy(index):
+        sibling = chan + 1 - 2 * lax.rem(chan, 2)
+        at = feat.at[block_at(index)]
+        return remote(at, at, pass_sem.at[index], feat_sem.at[index], (lat, lon, sibling))
+
+    def part_copy(index):
+        to_lat, to_lon = place(index)
+        return remote(
+            part.at[block_at(index)],
+            back.at[block_at(me)],
+            part_out_sem.at[index],
+            part_sem.at[me],
+            (to_lat, to_lon, chan),
+        )
+
+    def part_arrival(index):
+        at_lat, at_lon = place(index)
+        return remote(
+            part.at[block_at(index)],
+            back.at[block_at(index)],
+            part_out_sem.at[index],
+            part_sem.at[index],
+            (at_lat, at_lon, chan),
+        )
+
+    def one_block(step, carry):
+        index = lax.rem(me + step, group)
+        at = feat.at[block_at(index)]
+        is_own = (index == me) & (source_chan == chan)
+        local_copy = pltpu.make_async_copy(grad_out.at[0], at, feat_sem.at[index])
+        arrival = remote(at, at, pass_sem.at[index], feat_sem.at[index], (lat, lon, chan))
+        pl.when(is_own)(local_copy.wait)
+        pl.when(jnp.logical_not(is_own))(arrival.wait_recv)
+        pl.when(primary)(pass_copy(index).start)
+        product = jnp.dot(
+            feat[block_at(index), :], w_out[...], preferred_element_type=F32
+        ).astype(BF16)
+
+        @pl.when(index == me)
+        def _():
+            back[block_at(me), :] = product
+
+        @pl.when(index != me)
+        def _():
+            part[block_at(index), :] = product
+            part_copy(index).start()
+
+        return carry
+
+    lax.fori_loop(0, group, one_block, 0)
+    features_copy = pltpu.make_async_copy(feat, features, own_sem.at[2])
+    features_copy.start()
+
     allowed = allowed_pairs(
         valid[...], lat_first, lat_size * rows, rows, cols, slots, blocks, lon_size
     )
     spread = expand_bias(diag[...], cols, slots)
+    for copy in own_copies:
+        copy.wait()
+    for piece in rim_pieces():
+        for i in range(2):
+            pl.when(inside(-piece[2]))(kv_copy(piece, i).wait_recv)
+
+    def add_block(step, total):
+        index = lax.rem(me + step, group)
+        part_arrival(index).wait_recv()
+        return total + back[block_at(index), :].astype(F32)
+
+    own = back[block_at(me), :].astype(F32)
+    grad_attn[...] = lax.fori_loop(1, group, add_block, own).astype(BF16)
+
     for h in range(heads):
         at = pl.ds(h * HEAD_DIM, HEAD_DIM)
-        own = spread[h * blocks * cols : (h + 1) * blocks * cols]
+        head_bias = spread[h * blocks * cols : (h + 1) * blocks * cols]
         grad_q, grad_k, grad_v, folded = attend(
-            dims, allowed, own, q[:, at], g[:, at], kv[0, :, at], kv[1, :, at]
+            dims,
+            allowed,
+            head_bias,
+            q[:, at],
+            grad_attn[:, at],
+            kv[0, :, :, at].reshape(blocks * span, HEAD_DIM),
+            kv[1, :, :, at].reshape(blocks * span, HEAD_DIM),
         )
         gq[:, at] = grad_q.astype(BF16)
-        gkv[0, :, at] = grad_k
-        gkv[1, :, at] = grad_v
+        for i, grad in enumerate((grad_k, grad_v)):
+            gkv[i, :, at] = grad[rim : rim + tokens]
+            gsend[i, :, :, at] = grad.astype(BF16).reshape(blocks, span, HEAD_DIM)
         for b in range(blocks):
             fold[pl.ds((h * blocks + b) * cols, cols), :] = folded[b]
-    table[...] = collapse_bias(fold[...], cols, slots)
+
+    def grad_copy(piece, i):
+        b, d, shift, _, ext, _, from_lon = piece
+        dst = gmid.at[i, b] if d == 0 else grim.at[i, b, d - 1]
+        return remote(
+            gsend.at[i, b, pl.ds(*ext)],
+            dst,
+            g_out_sem.at[i, b, d],
+            g_sem.at[i, b, d],
+            (lat - shift, from_lon, chan),
+        )
+
+    for piece in rim_pieces():
+        for i in range(2):
+            pl.when(inside(-piece[2]))(grad_copy(piece, i).start)
+
+    tables[me] = collapse_bias(fold[...], cols, slots)
+
+    def table_copy(index, slot):
+        to_lat, to_lon = place(index)
+        return remote(
+            tables.at[me],
+            tables.at[slot],
+            t_out_sem.at[index],
+            t_sem.at[slot],
+            (to_lat, to_lon, chan),
+        )
+
+    def start_table(step, carry):
+        table_copy(lax.rem(me + step, group), me).start()
+        return carry
+
+    lax.fori_loop(1, group, start_table, 0)
+
+    for i in range(2):
+        for piece in rim_pieces():
+            b, d, shift, own, *_ = piece
+
+            @pl.when(inside(shift))
+            def _():
+                grad_copy(piece, i).wait_recv()
+                part_in = gmid[i, b] if d == 0 else grim[i, b, d - 1]
+                gkv[i, pl.ds(*own), :] = gkv[i, pl.ds(*own), :] + part_in.astype(F32)
+
+        (gk, gv)[i][...] = gkv[i].astype(BF16)
+
+    def add_table(step, total):
+        index = lax.rem(me + step, group)
+        table_copy(index, index).wait_recv()
+        return total + tables[index]
+
+    table[...] = lax.fori_loop(1, group, add_table, tables[me])
+
+    for i in range(slices):
+        for j in range(chan_size // 2):
+            away, out, _ = feature_copy(i, j)
+            pl.when(away)(out.wait_send)
+    for piece in rim_pieces():
+        for i in range(2):
+            pl.when(inside(piece[2]))(kv_copy(piece, i).wait_send)
+            pl.when(inside(-piece[2]))(grad_copy(piece, i).wait_send)
+
+    def sent(step, carry):
+        index = lax.rem(me + step, group)
+        pl.when(primary)(pass_copy(index).wait_send)
+
+        @pl.when(step > 0)
+        def _():
+            part_copy(index).wait_send()
+            table_copy(index, me).wait_send()
+
+        return carry
+
+    lax.fori_loop(0, group, sent, 0)
+    features_copy.wait()
 
 
 def diag_table(table, cols, slots, blocks, lon_size):
@@ -196,71 +499,72 @@
     rim = REACH * cols
     group = ("lat", "lon")
     dims = (rows, cols, slots, blocks)
-    whole = lax.all_gather(grad_out.reshape(tokens, -1), "chan", axis=1, tiled=True)
-    features = lax.all_to_all(whole, group, split_axis=1, concat_axis=0, tiled=True)
-    part = jnp.dot(features, w_out, preferred_element_type=F32).astype(BF16)
-    back = lax.all_to_all(part, group, split_axis=0, concat_axis=0, tiled=True)
-    grad_attn = jnp.sum(back.reshape(-1, tokens, width).astype(F32), axis=0).astype(BF16)
-
-    kv = jnp.stack([keys, values]).reshape(2, 1, tokens, width)
-    rights = [(i, (i + 1) % lon_size) for i in range(lon_size)]
-    lefts = [(j, i) for i, j in rights]
-    sides = [kv]
-    if blocks > 1:
-        sides.append(lax.ppermute(kv, "lon", lefts))
-    if blocks > 2:
-        sides.append(lax.ppermute(kv, "lon", rights))
-    kv = jnp.concatenate(sides, axis=1)
-    up = [(i, i + 1) for i in range(lat_size - 1)]
-    down = [(j, i) for i, j in up]
-    before = lax.ppermute(kv[:, :, tokens - rim :], "lat", up)
-    after = lax.ppermute(kv[:, :, :rim], "lat", down)
-    pad = jnp.zeros((2, blocks, span - tokens - 2 * rim, width), BF16)
-    kv = jnp.concatenate([before, kv, after, pad], axis=2).reshape(2, blocks * span, width)
-
+    depth = w_out.shape[0]
+    sizes = (lat_size, lon_size, lax.axis_size("chan"))
+    count = lat_size * lon_size
+    saved = lax.all_gather(attn_out.reshape(tokens, width), group, axis=0, tiled=True)
+    slices = grad_out.reshape(tokens, -1, depth).transpose(1, 0, 2)
     diag = diag_table(bias_table, cols, slots, blocks, lon_size)
     valid = valid_row(key_mask, rows, cols, slots, blocks, lon_size)
     vmem = pl.BlockSpec(memory_space=pltpu.VMEM)
-    grad_queries, grad_kv, diag_grad = pl.pallas_call(
-        functools.partial(attention_kernel, dims, lon_size, lat_size),
+    anywhere = pl.BlockSpec(memory_space=pl.ANY)
+    dma = pltpu.SemaphoreType.DMA
+    token = jax.ShapeDtypeStruct((tokens, width), BF16)
+    table_shape = (heads * blocks, slots * 2 * cols)
+    grad_queries, grad_keys, grad_values, diag_grad, features = pl.pallas_call(
+        functools.partial(mega_kernel, dims, sizes),
         out_shape=(
-            jax.ShapeDtypeStruct((tokens, width), BF16),
-            jax.ShapeDtypeStruct((2, blocks * span, width), F32),
-            jax.ShapeDtypeStruct((heads * blocks, slots * 2 * cols), F32),
+            token,
+            token,
+            token,
+            jax.ShapeDtypeStruct(table_shape, F32),
+            jax.ShapeDtypeStruct((count * tokens, depth), BF16),
         ),
-        in_specs=[vmem] * 5,
-        out_specs=(vmem,) * 3,
+        in_specs=[vmem] * 7,
+        out_specs=(vmem, vmem, vmem, vmem, anywhere),
         scratch_shapes=[
-            pltpu.VMEM((8, 128), F32),
+            pltpu.VMEM((2, blocks, span, width), BF16),
+            pltpu.VMEM((count * tokens, depth), BF16),
+            pltpu.VMEM((count * tokens, width), BF16),
+            pltpu.VMEM((count * tokens, width), BF16),
+            pltpu.VMEM((tokens, width), BF16),
+            pltpu.VMEM((2, tokens, width), F32),
+            pltpu.VMEM((2, blocks, span, width), BF16),
+            pltpu.VMEM((2, blocks, tokens, width), BF16),
+            pltpu.VMEM((2, blocks, 2, rim, width), BF16),
             pltpu.VMEM((heads * blocks * cols, span), F32),
+            pltpu.VMEM((count,) + table_shape, F32),
+            dma((slices.shape[0], sizes[2] // 2)),
+            dma((count,)),
+            dma((count,)),
+            dma((count,)),
+            dma((count,)),
+            dma((2, blocks, 3)),
+            dma((2, blocks, 3)),
+            dma((2, blocks, 3)),
+            dma((2, blocks, 3)),
+            dma((count,)),
+            dma((count,)),
+            dma((3,)),
         ],
-        compiler_params=pltpu.CompilerParams(vmem_limit_bytes=40 * 1024 * 1024),
-    )(valid, diag, queries.reshape(tokens, width), grad_attn, kv)
-
-    grad_kv = grad_kv.reshape(2, blocks, span, width)
-    own_before = lax.ppermute(grad_kv[:, :, :rim].astype(BF16), "lat", down).astype(F32)
-    own_after = lax.ppermute(
-        grad_kv[:, :, rim + tokens : 2 * rim + tokens].astype(BF16), "lat", up
-    ).astype(F32)
-    middle = grad_kv[:, :, rim : rim + tokens]
-    middle = (
-        middle
-        + jnp.pad(own_before, ((0, 0), (0, 0), (tokens - rim, 0), (0, 0)))
-        + jnp.pad(own_after, ((0, 0), (0, 0), (0, tokens - rim), (0, 0)))
-    )
-    total = middle[:, 0]
-    if blocks > 1:
-        total = total + lax.ppermute(middle[:, 1].astype(BF16), "lon", rights).astype(F32)
-    if blocks > 2:
-        total = total + lax.ppermute(middle[:, 2].astype(BF16), "lon", lefts).astype(F32)
-    total = total.astype(BF16).reshape(2, rows, cols, width)
-    diag_grad = lax.psum(diag_grad, group)
+        compiler_params=pltpu.CompilerParams(
+            collective_id=0, has_side_effects=True, vmem_limit_bytes=56 * 1024 * 1024
+        ),
+    )(
+        valid,
+        diag,
+        queries.reshape(tokens, width),
+        keys.reshape(tokens, width),
+        values.reshape(tokens, width),
+        slices,
+        w_out,
+    )
     grad_table = undiag_table(diag_grad, heads, cols, slots, blocks, lon_size)
-    saved = lax.all_gather(attn_out.reshape(tokens, width), group, axis=0, tiled=True)
     grad_wout = lax.dot_general(
         features, saved, (((0,), (0,)), ((), ())), preferred_element_type=F32
     )
-    return (grad_queries.reshape(rows, cols, width), total[0], total[1], grad_wout, grad_table)
+    tokens_out = [x.reshape(rows, cols, width) for x in (grad_queries, grad_keys, grad_values)]
+    return (*tokens_out, grad_wout, grad_table)
 
 
 def solution(mesh):

time: 204 us -> 143 us (0.70)
  the two profiles are of different devices: /device:TPU:0 before, /device:TPU:12 now
where the time goes in v2:
time: 143 us; the launch traced here: 142 us
  Pallas kernels  114 us (80%)
  between operations  14.1 us (10%)
  local copies, waits for them, and re-layouts  7.13 us (5%)
  matrix products  4.16 us (3%)
  other arithmetic  1.79 us (1%)
    pallas_call x1, Pallas kernels, local(): pl.pallas_call(functools.partial(mega_kernel, dims, sizes), out_shape=(to...  114 us
    dot_general x1, matrix products, local(): lax.dot_general(features, saved, (((0,), (0,)), ((), ())), preferred_elem...  4.16 us
    unnamed x13, local copies, waits for them, and re-layouts  2.87 us
  transfers between devices with their start and end apart: 1, of which 0 were waited for; matrix products, arithmetic and copies ran while one was open for 5% of the time, Pallas kernels for 80%

profile of v2, /device:TPU:12, one launch (start us, length us, event | category | flops | bytes accessed | tf_op | source)
XLA Modules:
  0.0 142.1 jit_solution(8619114127865389504)
XLA Ops:
  7.2 0.0 copy-start
  7.2 0.0 all-gather.2.cloned.1.call-start
  7.2 0.7 all-gather.2.cloned.1.call-update
  8.0 0.8 and_or_fusion
  8.7 0.1 pad_convert_fusion
  8.8 0.1 dynamic-slice_bitcast_fusion.1
  8.9 0.1 copy.17
  9.0 0.7 reshape.63.valid
  9.7 0.8 fusion.3
  10.5 0.8 add_bitcast_fusion
  11.3 0.1 copy.25
  11.5 0.7 reshape.64.diag
  12.2 0.0 copy-done
  12.2 0.1 reshape.68
  12.3 0.8 copy.27
  13.0 114.2 %shard_map.119 = (bf16[128,640]{1,0:T(8,128)(2,1)}, bf16[128,640]{1,0:T(8,128)(2,1)}, bf16[128,640]{1,0:T(8,128)(2,1)}, f32[10,512]{1,0:T(8,128)}, bf16[1024,640]{1,0:T(8,128)(2,1)}) custom-call(s32[1,512]{1,0:T(1,128)} %reshape.63.valid, f32[10,512]{1,0:T(8,128)} %reshape.64.diag, bf16[128,640]{1,0:T(8,128)(2,1)} %bitcast.36, bf16[128,640]{1,0:T(8,128)(2,1)} %bitcast.37, ...), custom_call_target="tpu_custom_call" | custom-call | tf_op jit(solution)/shard_map/pallas_call | solution.py:514
  127.2 0.9 reshape.73
  128.1 0.1 pad.30.clone
  128.1 0.1 slice_bitcast_fusion.1
  128.2 0.1 fusion
  128.4 0.7 copy.22
  129.1 0.0 all-gather.2.cloned.1.call-done
  129.1 0.0 copy-start.3
  129.1 0.0 copy-start.2
  129.1 0.0 copy-start.1
  129.1 4.2 %fusion.4 = f32[640,640]{1,0:T(8,128)} fusion(bf16[1024,640]{1,0:T(8,128)(2,1)} %get-tuple-element.13, bf16[1024,640]{1,0:T(8,128)(2,1)} %all-gather.2.cloned.1.call-done), kind=kOutput, calls=%fused_computation.18 | convolution fusion | flops 838860800 | bytes 4259840 | tf_op jit(solution)/shard_map/dot_general | solution.py:563
  133.2 0.0 copy-done.3
  133.3 0.7 copy.31
  133.9 0.0 copy-done.2
  133.9 0.7 copy.32
  134.6 0.0 copy-done.1
  134.6 0.7 copy.33
  (5 shorter events, 0.1 us)
Async XLA Ops:
  7.2 5.0 %copy-start = (bf16[16,8,1280]{2,1,0:T(8,128)(2,1)S(1)}, bf16[16,8,1280]{2,1,0:T(8,128)(2,1)}, u32[]{:S(2)}) copy-start(bf16[16,8,1280]{2,1,0:T(8,128)(2,1)} %param.12) | copy-start | bytes 983044
  7.2 121.9 %all-gather.2.cloned.1.call-start = ((), (), s32[]{:S(2)}) async-start(), calls=%async_computation | async-start | bytes 1474560 | tf_op jit(solution)/shard_map/all_gather | solution.py:505
  129.1 4.2 %copy-start.3 = (bf16[128,640]{1,0:T(8,128)(2,1)S(1)}, bf16[128,640]{1,0:T(8,128)(2,1)}, u32[]{:S(2)}) copy-start(bf16[128,640]{1,0:T(8,128)(2,1)} %get-tuple-element.10) | copy-start | bytes 491524
  129.1 4.8 %copy-start.2 = (bf16[128,640]{1,0:T(8,128)(2,1)S(1)}, bf16[128,640]{1,0:T(8,128)(2,1)}, u32[]{:S(2)}) copy-start(bf16[128,640]{1,0:T(8,128)(2,1)} %get-tuple-element.11) | copy-start | bytes 491524
  129.1 5.5 %copy-start.1 = (bf16[128,640]{1,0:T(8,128)(2,1)S(1)}, bf16[128,640]{1,0:T(8,128)(2,1)}, u32[]{:S(2)}) copy-start(bf16[128,640]{1,0:T(8,128)(2,1)} %get-tuple-element.12) | copy-start | bytes 491524
Sparse Core Ops, SparseCore 0:
  10.2 64.9 all-gather.1

commit v3 on v2

--- a/solution.py
+++ b/solution.py
@@ -130,17 +130,22 @@
     q,
     keys,
     values,
+    attn,
     grad_out,
     w_out,
     gq,
     gk,
     gv,
     table,
-    features,
+    wout,
     kv,
     feat,
     part,
+    side,
+    ready,
+    own_part,
     back,
+    saved,
     grad_attn,
     gkv,
     gsend,
@@ -152,7 +157,12 @@
     feat_sem,
     pass_sem,
     part_out_sem,
-    part_sem,
+    side_sem,
+    back_out_sem,
+    back_sem,
+    saved_out_sem,
+    saved_on_sem,
+    saved_sem,
     kv_out_sem,
     kv_sem,
     g_out_sem,
@@ -207,6 +217,8 @@
         pltpu.make_async_copy(x, kv.at[i, 0, pl.ds(rim, tokens)], own_sem.at[i])
         for i, x in enumerate((keys, values))
     ]
+    own_at = pl.ds(pl.multiple_of(me * tokens, tokens), tokens)
+    own_copies.append(pltpu.make_async_copy(attn, saved.at[own_at], own_sem.at[2]))
     for copy in own_copies:
         copy.start()
     pl.semaphore_wait(barrier, total_devices - 1)
@@ -223,13 +235,13 @@
         out = remote(
             src, dst, feat_out_sem.at[i, j], feat_sem.at[me], (to_lat, to_lon, to_chan)
         )
-        return away, out, pltpu.make_async_copy(src, dst, feat_sem.at[me])
+        return away, out, (src, dst, feat_sem.at[me])
 
     for i in range(slices):
         for j in range(chan_size // 2):
             away, out, own = feature_copy(i, j)
             pl.when(away)(out.start)
-            pl.when(jnp.logical_not(away))(own.start)
+            pl.when(jnp.logical_not(away))(lambda own=own: pltpu.make_async_copy(*own).start())
 
     def rim_pieces():
         pieces = []
@@ -290,24 +302,54 @@
         to_lat, to_lon = place(index)
         return remote(
             part.at[block_at(index)],
-            back.at[block_at(me)],
+            side.at[lon, to_lat],
             part_out_sem.at[index],
-            part_sem.at[me],
-            (to_lat, to_lon, chan),
-        )
-
-    def part_arrival(index):
-        at_lat, at_lon = place(index)
-        return remote(
-            part.at[block_at(index)],
-            back.at[block_at(index)],
-            part_out_sem.at[index],
-            part_sem.at[index],
-            (at_lat, at_lon, chan),
-        )
+            side_sem.at[lon, to_lat],
+            (lat, to_lon, chan),
+        )
+
+    def side_arrival(from_lon, row_block):
+        return remote(
+            side.at[from_lon, row_block],
+            side.at[from_lon, row_block],
+            part_out_sem.at[0],
+            side_sem.at[from_lon, row_block],
+            (lat, from_lon, chan),
+        )
+
+    def back_copy(row_block, slot):
+        return remote(
+            ready.at[row_block],
+            back.at[slot],
+            back_out_sem.at[row_block],
+            back_sem.at[slot],
+            (row_block, lon, chan),
+        )
+
+    def saved_copy(to_lat, slot):
+        return remote(
+            attn,
+            saved.at[block_at(slot)],
+            saved_out_sem.at[to_lat],
+            saved_sem.at[slot],
+            (to_lat, lon, chan),
+        )
+
+    def saved_pass(row_block, to_lon):
+        index = row_block * lon_size + lon
+        src = saved.at[block_at(index)]
+        return remote(
+            src, src, saved_on_sem.at[row_block, to_lon], saved_sem.at[index], (lat, to_lon, chan)
+        )
+
+    def saved_arrival(index):
+        at = saved.at[block_at(index)]
+        return remote(at, at, saved_out_sem.at[0], saved_sem.at[index], (lat, lon, chan))
 
     def one_block(step, carry):
-        index = lax.rem(me + step, group)
+        at_lat = lax.rem(lat + 1 + step // lon_size, lat_size)
+        at_lon = lax.rem(lon + 1 + lax.rem(step, lon_size), lon_size)
+        index = at_lat * lon_size + at_lon
         at = feat.at[block_at(index)]
         is_own = (index == me) & (source_chan == chan)
         local_copy = pltpu.make_async_copy(grad_out.at[0], at, feat_sem.at[index])
@@ -317,22 +359,47 @@
         pl.when(primary)(pass_copy(index).start)
         product = jnp.dot(
             feat[block_at(index), :], w_out[...], preferred_element_type=F32
-        ).astype(BF16)
-
-        @pl.when(index == me)
+        )
+
+        part[block_at(index), :] = product.astype(BF16)
+
+        @pl.when(at_lon == lon)
         def _():
-            back[block_at(me), :] = product
-
-        @pl.when(index != me)
+            own_part[at_lat] = product
+
+        @pl.when(at_lon != lon)
         def _():
-            part[block_at(index), :] = product
             part_copy(index).start()
 
         return carry
 
     lax.fori_loop(0, group, one_block, 0)
-    features_copy = pltpu.make_async_copy(feat, features, own_sem.at[2])
-    features_copy.start()
+
+    def one_sum(step, carry):
+        row_block = lax.rem(lat + step, lat_size)
+
+        def add_side(turn, total):
+            from_lon = lax.rem(lon + turn, lon_size)
+            side_arrival(from_lon, row_block).wait_recv()
+            return total + side[from_lon, row_block].astype(F32)
+
+        total = lax.fori_loop(1, lon_size, add_side, own_part[row_block])
+        own_part[row_block] = total
+
+        @pl.when(row_block != lat)
+        def _():
+            ready[row_block] = total.astype(BF16)
+            back_copy(row_block, lat).start()
+
+        return carry
+
+    lax.fori_loop(1, lat_size + 1, one_sum, 0)
+
+    def start_saved(step, carry):
+        saved_copy(lax.rem(lat + step, lat_size), me).start()
+        return carry
+
+    lax.fori_loop(1, lat_size, start_saved, 0)
 
     allowed = allowed_pairs(
         valid[...], lat_first, lat_size * rows, rows, cols, slots, blocks, lon_size
@@ -345,12 +412,11 @@
             pl.when(inside(-piece[2]))(kv_copy(piece, i).wait_recv)
 
     def add_block(step, total):
-        index = lax.rem(me + step, group)
-        part_arrival(index).wait_recv()
-        return total + back[block_at(index), :].astype(F32)
-
-    own = back[block_at(me), :].astype(F32)
-    grad_attn[...] = lax.fori_loop(1, group, add_block, own).astype(BF16)
+        row_block = lax.rem(lat + step, lat_size)
+        back_copy(row_block, row_block).wait_recv()
+        return total + back[row_block].astype(F32)
+
+    grad_attn[...] = lax.fori_loop(1, lat_size, add_block, own_part[lat]).astype(BF16)
 
     for h in range(heads):
         at = pl.ds(h * HEAD_DIM, HEAD_DIM)
@@ -404,6 +470,21 @@
 
     lax.fori_loop(1, group, start_table, 0)
 
+    def pass_saved(step, carry):
+        row_block = lax.rem(lat + step, lat_size)
+
+        @pl.when(step > 0)
+        def _():
+            saved_arrival(row_block * lon_size + lon).wait_recv()
+
+        def to_side(turn, carry):
+            saved_pass(row_block, lax.rem(lon + turn, lon_size)).start()
+            return carry
+
+        return lax.fori_loop(1, lon_size, to_side, carry)
+
+    lax.fori_loop(0, lat_size, pass_saved, 0)
+
     for i in range(2):
         for piece in rim_pieces():
             b, d, shift, own, *_ = piece
@@ -422,6 +503,23 @@
         return total + tables[index]
 
     table[...] = lax.fori_loop(1, group, add_table, tables[me])
+
+    def await_saved(step, carry):
+        row_block, turn = step // (lon_size - 1), lax.rem(step, lon_size - 1)
+        from_lon = lax.rem(lon + 1 + turn, lon_size)
+        saved_arrival(row_block * lon_size + from_lon).wait_recv()
+        return carry
+
+    if lon_size > 1:
+        lax.fori_loop(0, lat_size * (lon_size - 1), await_saved, 0)
+    strip = 128 if width % 128 == 0 else width
+    for start in range(0, width, strip):
+        wout[:, pl.ds(start, strip)] = lax.dot_general(
+            feat[...],
+            saved[:, pl.ds(start, strip)],
+            (((0,), (0,)), ((), ())),
+            preferred_element_type=F32,
+        )
 
     for i in range(slices):
         for j in range(chan_size // 2):
@@ -436,15 +534,28 @@
         index = lax.rem(me + step, group)
         pl.when(primary)(pass_copy(index).wait_send)
 
+        _, at_lon = place(index)
+
+        @pl.when(at_lon != lon)
+        def _():
+            part_copy(index).wait_send()
+            saved_pass(index // lon_size, at_lon).wait_send()
+
         @pl.when(step > 0)
         def _():
-            part_copy(index).wait_send()
             table_copy(index, me).wait_send()
 
         return carry
 
     lax.fori_loop(0, group, sent, 0)
-    features_copy.wait()
+
+    def sent_rows(step, carry):
+        row_block = lax.rem(lat + step, lat_size)
+        back_copy(row_block, lat).wait_send()
+        saved_copy(row_block, me).wait_send()
+        return carry
+
+    lax.fori_loop(1, lat_size, sent_rows, 0)
 
 
 def diag_table(table, cols, slots, blocks, lon_size):
@@ -502,30 +613,32 @@
     depth = w_out.shape[0]
     sizes = (lat_size, lon_size, lax.axis_size("chan"))
     count = lat_size * lon_size
-    saved = lax.all_gather(attn_out.reshape(tokens, width), group, axis=0, tiled=True)
     slices = grad_out.reshape(tokens, -1, depth).transpose(1, 0, 2)
     diag = diag_table(bias_table, cols, slots, blocks, lon_size)
     valid = valid_row(key_mask, rows, cols, slots, blocks, lon_size)
     vmem = pl.BlockSpec(memory_space=pltpu.VMEM)
-    anywhere = pl.BlockSpec(memory_space=pl.ANY)
     dma = pltpu.SemaphoreType.DMA
     token = jax.ShapeDtypeStruct((tokens, width), BF16)
     table_shape = (heads * blocks, slots * 2 * cols)
-    grad_queries, grad_keys, grad_values, diag_grad, features = pl.pallas_call(
+    grad_queries, grad_keys, grad_values, diag_grad, grad_wout = pl.pallas_call(
         functools.partial(mega_kernel, dims, sizes),
         out_shape=(
             token,
             token,
             token,
             jax.ShapeDtypeStruct(table_shape, F32),
-            jax.ShapeDtypeStruct((count * tokens, depth), BF16),
+            jax.ShapeDtypeStruct((depth, width), F32),
         ),
-        in_specs=[vmem] * 7,
-        out_specs=(vmem, vmem, vmem, vmem, anywhere),
+        in_specs=[vmem] * 8,
+        out_specs=(vmem,) * 5,
         scratch_shapes=[
             pltpu.VMEM((2, blocks, span, width), BF16),
             pltpu.VMEM((count * tokens, depth), BF16),
             pltpu.VMEM((count * tokens, width), BF16),
+            pltpu.VMEM((lon_size, lat_size, tokens, width), BF16),
+            pltpu.VMEM((lat_size, tokens, width), BF16),
+            pltpu.VMEM((lat_size, tokens, width), F32),
+            pltpu.VMEM((lat_size, tokens, width), BF16),
             pltpu.VMEM((count * tokens, width), BF16),
             pltpu.VMEM((tokens, width), BF16),
             pltpu.VMEM((2, tokens, width), F32),
@@ -538,6 +651,11 @@
             dma((count,)),
             dma((count,)),
             dma((count,)),
+            dma((lon_size, lat_size)),
+            dma((lat_size,)),
+            dma((lat_size,)),
+            dma((lat_size,)),
+            dma((lat_size, lon_size)),
             dma((count,)),
             dma((2, blocks, 3)),
             dma((2, blocks, 3)),
@@ -556,13 +674,11 @@
         queries.reshape(tokens, width),
         keys.reshape(tokens, width),
         values.reshape(tokens, width),
+        attn_out.reshape(tokens, width),
         slices,
         w_out,
     )
     grad_table = undiag_table(diag_grad, heads, cols, slots, blocks, lon_size)
-    grad_wout = lax.dot_general(
-        features, saved, (((0,), (0,)), ((), ())), preferred_element_type=F32
-    )
     tokens_out = [x.reshape(rows, cols, width) for x in (grad_queries, grad_keys, grad_values)]
     return (*tokens_out, grad_wout, grad_table)
 

time: 143 us -> 115 us (0.80)
  between operations: 14.1 us -> 0.72 us
  Pallas kernels: 114 us -> 101 us
  matrix products: 4.16 us -> 0 us
  local copies, waits for them, and re-layouts: 7.13 us -> 11.2 us
    pallas_call x1, Pallas kernels: 114 us -> 101 us  [local(): pl.pallas_call(functools.partial(mega_kernel, dims, sizes), out_shape=(to...]
    dot_general x1 -> x0, matrix products: 4.16 us -> none  [local(): lax.dot_general(features, saved, (((0,), (0,)), ((), ())), preferred_elem...]
    unnamed x13 -> x10, local copies, waits for them, and re-layouts: 2.87 us -> 6.81 us
  transfers between devices with their start and end apart: 1 -> 0, of which waited for: 0 -> 0; matrix products, arithmetic and copies ran while one was open for 5% -> 0% of each run, Pallas kernels for 80% -> 0%
where the time goes in v3:
time: 115 us
  Pallas kernels  101 us (88%)
  local copies, waits for them, and re-layouts  11.2 us (10%)
  other arithmetic  1.83 us (2%)
    pallas_call x1, Pallas kernels, local(): pl.pallas_call(functools.partial(mega_kernel, dims, sizes), out_shape=(to...  101 us
    unnamed x10, local copies, waits for them, and re-layouts  6.81 us

profile of v3, /device:TPU:12, one launch (start us, length us, event | category | flops | bytes accessed | tf_op | source)
XLA Modules:
  0.0 114.6 jit_solution(3176967460349519873)
XLA Ops:
  0.6 0.0 copy-start.1
  0.7 0.8 and_or_fusion
  1.5 0.1 pad_convert_fusion
  1.6 0.1 dynamic-slice_bitcast_fusion.1
  1.6 0.1 copy.17
  1.7 0.7 reshape.63.valid
  2.4 0.8 fusion.3
  3.2 0.8 add_bitcast_fusion
  4.0 0.1 copy.25
  4.2 0.7 reshape.64.diag
  4.9 0.0 copy-done.1
  4.9 0.1 reshape.69
  5.0 0.8 copy.27
  5.8 100.8 %shard_map.119 = (bf16[128,640]{1,0:T(8,128)(2,1)}, bf16[128,640]{1,0:T(8,128)(2,1)}, bf16[128,640]{1,0:T(8,128)(2,1)}, f32[10,512]{1,0:T(8,128)}, f32[640,640]{1,0:T(8,128)}) custom-call(s32[1,512]{1,0:T(1,128)} %reshape.63.valid, f32[10,512]{1,0:T(8,128)} %reshape.64.diag, bf16[128,640]{1,0:T(8,128)(2,1)} %bitcast.37, bf16[128,640]{1,0:T(8,128)(2,1)} %bitcast.38, ...), custom_call_target="tpu_custom_call" | custom-call | tf_op jit(solution)/shard_map/pallas_call | solution.py:623
  106.6 0.0 copy-start
  106.6 1.0 reshape.73
  107.6 0.1 slice_bitcast_fusion.1
  107.7 0.1 pad.30.clone
  107.8 0.1 fusion
  107.9 0.7 copy.22
  108.6 1.6 %copy.32 = bf16[16,8,640]{2,1,0:T(8,128)(2,1)} copy(bf16[16,8,640]{2,1,0:T(8,128)(2,1)} %bitcast.36) | data formatting | bytes 327680
  110.2 1.6 %copy.33 = bf16[16,8,640]{2,1,0:T(8,128)(2,1)} copy(bf16[16,8,640]{2,1,0:T(8,128)(2,1)} %bitcast.35) | data formatting | bytes 327680
  111.8 1.6 %copy.34 = bf16[16,8,640]{2,1,0:T(8,128)(2,1)} copy(bf16[16,8,640]{2,1,0:T(8,128)(2,1)} %bitcast.34) | data formatting | bytes 327680
  113.4 0.0 copy-done
  113.4 1.2 %copy.35 = f32[640,640]{1,0:T(8,128)} copy(f32[640,640]{1,0:T(8,128)S(1)} %copy-done) | data formatting | bytes 3276800
  (5 shorter events, 0.1 us)
Async XLA Ops:
  0.6 4.3 %copy-start.1 = (bf16[16,8,1280]{2,1,0:T(8,128)(2,1)S(1)}, bf16[16,8,1280]{2,1,0:T(8,128)(2,1)}, u32[]{:S(2)}) copy-start(bf16[16,8,1280]{2,1,0:T(8,128)(2,1)} %param.12) | copy-start | bytes 983044
  106.6 6.8 %copy-start = (f32[640,640]{1,0:T(8,128)S(1)}, f32[640,640]{1,0:T(8,128)}, u32[]{:S(2)}) copy-start(f32[640,640]{1,0:T(8,128)} %get-tuple-element.36) | copy-start | bytes 4915204

commit v4 on v3

--- a/solution.py
+++ b/solution.py
@@ -156,6 +156,7 @@
     feat_out_sem,
     feat_sem,
     pass_sem,
+    relay_sem,
     part_out_sem,
     side_sem,
     back_out_sem,
@@ -229,8 +230,7 @@
     def feature_copy(i, j):
         target = chan * slices + i
         to_lat, to_lon = place(target)
-        to_chan = 2 * j + lax.rem(chan, 2)
-        away = (target != me) | (to_chan != chan)
+        to_chan, away = chan, target != me
         src, dst = grad_out.at[i], feat.at[block_at(me)]
         out = remote(
             src, dst, feat_out_sem.at[i, j], feat_sem.at[me], (to_lat, to_lon, to_chan)
@@ -238,7 +238,7 @@
         return away, out, (src, dst, feat_sem.at[me])
 
     for i in range(slices):
-        for j in range(chan_size // 2):
+        for j in range(1):
             away, out, own = feature_copy(i, j)
             pl.when(away)(out.start)
             pl.when(jnp.logical_not(away))(lambda own=own: pltpu.make_async_copy(*own).start())
@@ -291,7 +291,37 @@
                 kv[i, b, pl.ds(rim + tokens, rim), :] = jnp.zeros((rim, width), BF16)
 
     lat_first = lat * rows
+    def saved_copy(to_lat, slot):
+        return remote(
+            attn,
+            saved.at[block_at(slot)],
+            saved_out_sem.at[to_lat],
+            saved_sem.at[slot],
+            (to_lat, lon, chan),
+        )
+
+    def saved_pass(row_block, to_lon):
+        index = row_block * lon_size + lon
+        src = saved.at[block_at(index)]
+        return remote(
+            src, src, saved_on_sem.at[row_block, to_lon], saved_sem.at[index], (lat, to_lon, chan)
+        )
+
+    def saved_arrival(index):
+        at = saved.at[block_at(index)]
+        return remote(at, at, saved_out_sem.at[0], saved_sem.at[index], (lat, lon, chan))
+
     primary = lax.rem(source_chan, 2) == lax.rem(chan, 2)
+    def start_saved(step, carry):
+        saved_copy(lax.rem(lat + step, lat_size), me).start()
+        return carry
+
+    lax.fori_loop(1, lat_size, start_saved, 0)
+
+    def relay_copy(index, j):
+        at = feat.at[block_at(index)]
+        to_chan = lax.rem(chan + 2 * j, chan_size)
+        return remote(at, at, relay_sem.at[index, j], feat_sem.at[index], (lat, lon, to_chan))
 
     def pass_copy(index):
         sibling = chan + 1 - 2 * lax.rem(chan, 2)
@@ -325,26 +355,6 @@
             back_sem.at[slot],
             (row_block, lon, chan),
         )
-
-    def saved_copy(to_lat, slot):
-        return remote(
-            attn,
-            saved.at[block_at(slot)],
-            saved_out_sem.at[to_lat],
-            saved_sem.at[slot],
-            (to_lat, lon, chan),
-        )
-
-    def saved_pass(row_block, to_lon):
-        index = row_block * lon_size + lon
-        src = saved.at[block_at(index)]
-        return remote(
-            src, src, saved_on_sem.at[row_block, to_lon], saved_sem.at[index], (lat, to_lon, chan)
-        )
-
-    def saved_arrival(index):
-        at = saved.at[block_at(index)]
-        return remote(at, at, saved_out_sem.at[0], saved_sem.at[index], (lat, lon, chan))
 
     def one_block(step, carry):
         at_lat = lax.rem(lat + 1 + step // lon_size, lat_size)
@@ -357,6 +367,8 @@
         pl.when(is_own)(local_copy.wait)
         pl.when(jnp.logical_not(is_own))(arrival.wait_recv)
         pl.when(primary)(pass_copy(index).start)
+        for j in range(1, chan_size // 2):
+            pl.when(source_chan == chan)(relay_copy(index, j).start)
         product = jnp.dot(
             feat[block_at(index), :], w_out[...], preferred_element_type=F32
         )
@@ -394,19 +406,28 @@
         return carry
 
     lax.fori_loop(1, lat_size + 1, one_sum, 0)
-
-    def start_saved(step, carry):
-        saved_copy(lax.rem(lat + step, lat_size), me).start()
-        return carry
-
-    lax.fori_loop(1, lat_size, start_saved, 0)
+    for copy in own_copies:
+        copy.wait()
+    def pass_saved(step, carry):
+        row_block = lax.rem(lat + step, lat_size)
+
+        @pl.when(step > 0)
+        def _():
+            saved_arrival(row_block * lon_size + lon).wait_recv()
+
+        def to_side(turn, carry):
+            saved_pass(row_block, lax.rem(lon + turn, lon_size)).start()
+            return carry
+
+        return lax.fori_loop(1, lon_size, to_side, carry)
+
+    lax.fori_loop(0, lat_size, pass_saved, 0)
+
 
     allowed = allowed_pairs(
         valid[...], lat_first, lat_size * rows, rows, cols, slots, blocks, lon_size
     )
     spread = expand_bias(diag[...], cols, slots)
-    for copy in own_copies:
-        copy.wait()
     for piece in rim_pieces():
         for i in range(2):
             pl.when(inside(-piece[2]))(kv_copy(piece, i).wait_recv)
@@ -470,20 +491,6 @@
 
     lax.fori_loop(1, group, start_table, 0)
 
-    def pass_saved(step, carry):
-        row_block = lax.rem(lat + step, lat_size)
-
-        @pl.when(step > 0)
-        def _():
-            saved_arrival(row_block * lon_size + lon).wait_recv()
-
-        def to_side(turn, carry):
-            saved_pass(row_block, lax.rem(lon + turn, lon_size)).start()
-            return carry
-
-        return lax.fori_loop(1, lon_size, to_side, carry)
-
-    lax.fori_loop(0, lat_size, pass_saved, 0)
 
     for i in range(2):
         for piece in rim_pieces():
@@ -522,7 +529,7 @@
         )
 
     for i in range(slices):
-        for j in range(chan_size // 2):
+        for j in range(1):
             away, out, _ = feature_copy(i, j)
             pl.when(away)(out.wait_send)
     for piece in rim_pieces():
@@ -533,6 +540,8 @@
     def sent(step, carry):
         index = lax.rem(me + step, group)
         pl.when(primary)(pass_copy(index).wait_send)
+        for j in range(1, chan_size // 2):
+            pl.when(source_chan == chan)(relay_copy(index, j).wait_send)
 
         _, at_lon = place(index)
 
@@ -650,6 +659,7 @@
             dma((slices.shape[0], sizes[2] // 2)),
             dma((count,)),
             dma((count,)),
+            dma((count, sizes[2] // 2)),
             dma((count,)),
             dma((lon_size, lat_size)),
             dma((lat_size,)),

time: 115 us -> 96.3 us (0.84)
  Pallas kernels: 101 us -> 82.2 us
    pallas_call x1, Pallas kernels: 101 us -> 82.2 us  [local(): pl.pallas_call(functools.partial(mega_kernel, dims, sizes), out_shape=(to...]
where the time goes in v4:
time: 96.3 us; the launch traced here: 96 us
  Pallas kernels  82.2 us (85%)
  local copies, waits for them, and re-layouts  11.2 us (12%)
  other arithmetic  1.83 us (2%)
    pallas_call x1, Pallas kernels, local(): pl.pallas_call(functools.partial(mega_kernel, dims, sizes), out_shape=(to...  82.2 us
    unnamed x10, local copies, waits for them, and re-layouts  6.81 us

profile of v4, /device:TPU:12, one launch (start us, length us, event | category | flops | bytes accessed | tf_op | source)
XLA Modules:
  0.0 96.0 jit_solution(6381374563451151838)
XLA Ops:
  0.6 0.0 copy-start.1
  0.7 0.8 and_or_fusion
  1.5 0.1 pad_convert_fusion
  1.6 0.1 dynamic-slice_bitcast_fusion.1
  1.6 0.1 copy.17
  1.7 0.7 reshape.63.valid
  2.4 0.8 fusion.3
  3.2 0.8 add_bitcast_fusion
  4.0 0.1 copy.25
  4.2 0.7 reshape.64.diag
  4.9 0.0 copy-done.1
  4.9 0.1 reshape.69
  5.0 0.8 copy.27
  5.8 82.2 %shard_map.119 = (bf16[128,640]{1,0:T(8,128)(2,1)}, bf16[128,640]{1,0:T(8,128)(2,1)}, bf16[128,640]{1,0:T(8,128)(2,1)}, f32[10,512]{1,0:T(8,128)}, f32[640,640]{1,0:T(8,128)}) custom-call(s32[1,512]{1,0:T(1,128)} %reshape.63.valid, f32[10,512]{1,0:T(8,128)} %reshape.64.diag, bf16[128,640]{1,0:T(8,128)(2,1)} %bitcast.37, bf16[128,640]{1,0:T(8,128)(2,1)} %bitcast.38, ...), custom_call_target="tpu_custom_call" | custom-call | tf_op jit(solution)/shard_map/pallas_call | solution.py:632
  88.0 0.0 copy-start
  88.0 1.0 %reshape.73 = f32[5,2,32,16]{3,2,1,0:T(8,128)S(1)} reshape(f32[10,512]{1,0:T(8,128)} %get-tuple-element.14) | data formatting | bytes 40960 | tf_op jit(solution)/shard_map/reshape | solution.py:586
  89.0 0.1 slice_bitcast_fusion.1
  89.1 0.1 pad.30.clone
  89.2 0.1 fusion
  89.3 0.7 copy.22
  90.0 1.6 %copy.32 = bf16[16,8,640]{2,1,0:T(8,128)(2,1)} copy(bf16[16,8,640]{2,1,0:T(8,128)(2,1)} %bitcast.36) | data formatting | bytes 327680
  91.6 1.6 %copy.33 = bf16[16,8,640]{2,1,0:T(8,128)(2,1)} copy(bf16[16,8,640]{2,1,0:T(8,128)(2,1)} %bitcast.35) | data formatting | bytes 327680
  93.2 1.6 %copy.34 = bf16[16,8,640]{2,1,0:T(8,128)(2,1)} copy(bf16[16,8,640]{2,1,0:T(8,128)(2,1)} %bitcast.34) | data formatting | bytes 327680
  94.8 0.0 copy-done
  94.8 1.2 %copy.35 = f32[640,640]{1,0:T(8,128)} copy(f32[640,640]{1,0:T(8,128)S(1)} %copy-done) | data formatting | bytes 3276800
  (5 shorter events, 0.1 us)
Async XLA Ops:
  0.6 4.3 %copy-start.1 = (bf16[16,8,1280]{2,1,0:T(8,128)(2,1)S(1)}, bf16[16,8,1280]{2,1,0:T(8,128)(2,1)}, u32[]{:S(2)}) copy-start(bf16[16,8,1280]{2,1,0:T(8,128)(2,1)} %param.12) | copy-start | bytes 983044
  88.0 6.8 %copy-start = (f32[640,640]{1,0:T(8,128)S(1)}, f32[640,640]{1,0:T(8,128)}, u32[]{:S(2)}) copy-start(f32[640,640]{1,0:T(8,128)} %get-tuple-element.36) | copy-start | bytes 4915204
